TPU v7x, 256 devices: a whole 4x4x8 slice. The times are simulated.
256 devices in a mesh: gx: 16 (over y_hi, z), gy: 16 (over x, y_lo, core).
Axes of the slice: x: 4, y: 4 (y_hi: 2, y_lo: 2; y = y_hi * 2 + y_lo), z: 8, core: 2. Of those that a mesh axis runs over, the one named last changes fastest.
Arguments:
- fine_solution: float32 [512, 512, 512], P('gx', 'gy'), may hold values from -6 to 6
- fine_source: float32 [512, 512, 512], P('gx', 'gy'), may hold values from -6 to 6
- fine_coef: float32 [512, 512, 512], P('gx', 'gy'), may hold values from 0.25 to 4
- coarse_correction: float32 [256, 256, 256], P('gx', 'gy'), may hold values from -6 to 6
- coarse_source: float32 [256, 256, 256], P('gx', 'gy'), may hold values from -6 to 6
- coarse_coef: float32 [256, 256, 256], P('gx', 'gy'), may hold values from 0.25 to 4
Outputs:
- fine_next: float32 [512, 512, 512], P('gx', 'gy')
- restricted: float32 [256, 256, 256], P('gx', 'gy')
- coarse_next: float32 [256, 256, 256], P('gx', 'gy')
All inputs are finite; a program needn't handle non-finite values.
Results may differ from a plain program's by a relative error of at most 0.00015.
Values sent between devices are 32-bit elements; how exact they have to be, the bound alone decides.
No kernel may reach another device: no remote copies, remote signals or barrier semaphores. Data moves between devices by JAX's collectives and lax.ppermute only.
A program may use at most 128 MiB of HBM per device.

v0:
```python
import functools

import jax
import jax.numpy as jnp
from jax import lax
from jax.experimental import pallas as pl
from jax.experimental.pallas import tpu as pltpu
from jax.sharding import PartitionSpec as P

MASS = 0.2
THETA = 1.125
DELTA = 0.875
SIGMA = THETA / DELTA
STEPS = 4
F32 = jnp.float32

NF, ZF, TF = 32, 512, 5
NC, ZC, TC = 16, 256, 3
XROWS = 11 * NF + 11 * 8
YROWS = 8 * (NF + NF // 2 + 12)
LIMIT = 56 * 1024 * 1024


def step_factors():
    ratio = 1.0 / SIGMA
    factors = []
    for _ in range(STEPS - 1):
        following = 1.0 / (2.0 * SIGMA - ratio)
        factors.append((following * ratio, 2.0 * following / DELTA))
        ratio = following
    return factors


def upper_rows(shape):
    return lax.broadcasted_iota(jnp.int32, shape, len(shape) - 2) < 4


def turn(block):
    return pltpu.roll(block, 4, axis=block.ndim - 2)


def pair_up(first, second):
    return jnp.where(upper_rows(first.shape), first, turn(second))


def pair_down(first, second):
    return jnp.where(upper_rows(first.shape), turn(second), first)


def halo_first(up, down):
    return jnp.where(upper_rows(up.shape), up, down)


def halo_second(up, down):
    return turn(jnp.where(upper_rows(up.shape), down, up))


def pack_kernel(
    u_lo, u_hi, c_lo, c_hi, f_lo, f_hi,
    u_r0, u_r3, c_r0, c_r3, f_r0, f_r3,
    e, cc, cs, x_lo, x_hi, y_up, y_dn,
):
    k = 0
    for lo, hi, coarse, count in ((u_lo, u_hi, e, 4), (c_lo, c_hi, cc, 4), (f_lo, f_hi, cs, 3)):
        for j in range(count):
            dist = count - 1 - j
            x_lo[NF * k : NF * (k + 1), :] = lo[dist]
            x_hi[NF * k : NF * (k + 1), :] = hi[3 - dist]
            row = 11 * NF + 8 * k
            for half in range(2):
                lanes = slice(ZC * half, ZC * (half + 1))
                rows = slice(8 * half, 8 * (half + 1))
                x_lo[row : row + 8, lanes] = coarse[dist, rows, :]
                x_hi[row : row + 8, lanes] = coarse[NC - 1 - dist, rows, :]
            k += 1

    for x in range(NF):
        y_up[8 * x : 8 * x + 8, :] = pair_up(u_r0[x], c_r0[x])
        y_dn[8 * x : 8 * x + 8, :] = pair_down(u_r3[x], c_r3[x])
    for m in range(NF // 2):
        row = 8 * (NF + m)
        y_up[row : row + 8, :] = pair_up(f_r0[2 * m], f_r0[2 * m + 1])
        y_dn[row : row + 8, :] = pair_down(f_r3[2 * m], f_r3[2 * m + 1])
    for h in range(NC + NC // 2):
        row = 8 * (NF + NF // 2 + h // 2)
        lanes = slice(ZC * (h % 2), ZC * (h % 2 + 1))
        if h < NC:
            pair = ((e, h), (cc, h))
        else:
            pair = ((cs, 2 * (h - NC)), (cs, 2 * (h - NC) + 1))
        low = [ref[i, 0:8, :] for ref, i in pair]
        high = [ref[i, 8:16, :] for ref, i in pair]
        y_up[row : row + 8, lanes] = pair_up(*low)
        y_dn[row : row + 8, lanes] = pair_down(*high)


def pack(u, c, f, e, cc, cs):
    def face(side):
        return pl.BlockSpec((4, NF, ZF), lambda i: (7 * side, 0, 0))

    def strip(at):
        return pl.BlockSpec((NF, 8, ZF), lambda i: (0, at, 0))

    whole = pl.BlockSpec((NC, NC, ZC), lambda i: (0, 0, 0))
    x_spec = pl.BlockSpec((XROWS, ZF), lambda i: (0, 0))
    y_spec = pl.BlockSpec((YROWS, ZF), lambda i: (0, 0))
    return pl.pallas_call(
        pack_kernel,
        grid=(1,),
        in_specs=[face(0), face(1)] * 3 + [strip(0), strip(3)] * 3 + [whole] * 3,
        out_specs=[x_spec, x_spec, y_spec, y_spec],
        out_shape=[jax.ShapeDtypeStruct((XROWS, ZF), F32)] * 2
        + [jax.ShapeDtypeStruct((YROWS, ZF), F32)] * 2,
        compiler_params=pltpu.CompilerParams(vmem_limit_bytes=LIMIT),
        name="pack_faces",
    )(u, u, c, c, f, f, u, u, c, c, f, f, e, cc, cs)


class Slab:
    def __init__(self, planes, tiles, depth, scale, refs):
        self.n, self.t, self.z, self.scale = planes, tiles, depth, scale
        self.lanes = depth // 128
        (
            self.u, self.c, self.f, self.p, self.q, self.total,
            self.wx, self.wy, self.wz, self.inv, self.flux, self.plane,
        ) = refs

    @staticmethod
    def scratch(planes, tiles, depth):
        rows, lanes = 8 * tiles, depth // 128
        split = pltpu.VMEM((planes, lanes, rows, 128), F32)
        whole = pltpu.VMEM((planes, rows, depth), F32)
        return [split] * 3 + [whole] * 7 + [
            pltpu.VMEM((rows, depth), F32),
            pltpu.VMEM((lanes, rows, 128), F32),
        ]

    def tile(self, ref, x, t):
        parts = [ref[x, j, pl.ds(t, 8, stride=self.t), :] for j in range(self.lanes)]
        return jnp.concatenate(parts, axis=1)

    def tiles(self, ref, x):
        return [self.tile(ref, x, t) for t in range(self.t)]

    def rows(self, t):
        return slice(8 * t, 8 * t + 8)

    def put_halo(self, ref, x, block):
        top = 8 * (self.t - 1)
        for j in range(self.lanes):
            ref[x, j, top : top + 8, :] = block[:, 128 * j : 128 * (j + 1)]

    def put_own(self, ref, x, block):
        own = 8 * (self.t - 1)
        for j in range(self.lanes):
            ref[x, j, 0:own, :] = block[:, 128 * j : 128 * (j + 1)]

    def next_row(self, values):
        return values[1:] + [pltpu.roll(values[0], 7, axis=0)]

    def last_row(self, values):
        return [pltpu.roll(values[-1], 1, axis=0)] + values[:-1]

    def next_deep(self, value):
        return pltpu.roll(value, self.z - 1, axis=1)

    def last_deep(self, value):
        return pltpu.roll(value, 1, axis=1)

    def first_pass(self):
        half = 0.5 * self.scale
        u0, u1 = self.tiles(self.u, 0), self.tiles(self.u, 1)
        c0, c1 = self.tiles(self.c, 0), self.tiles(self.c, 1)
        for t in range(self.t):
            w = half * (c0[t] + c1[t])
            self.wx[0, self.rows(t), :] = w
            self.flux[self.rows(t), :] = w * (u1[t] - u0[t])

        def body(x, carry):
            u, c = self.tiles(self.u, x), self.tiles(self.c, x)
            u_row, c_row = self.next_row(u), self.next_row(c)
            wy = [half * (c[t] + c_row[t]) for t in range(self.t)]
            fy = [wy[t] * (u_row[t] - u[t]) for t in range(self.t)]
            wy_last, fy_last = self.last_row(wy), self.last_row(fy)
            for t in range(self.t):
                rows = self.rows(t)
                wx = half * (c[t] + self.tile(self.c, x + 1, t))
                wz = half * (c[t] + self.next_deep(c[t]))
                fx = wx * (self.tile(self.u, x + 1, t) - u[t])
                fz = wz * (self.next_deep(u[t]) - u[t])
                faces = (wx + self.wx[x - 1, rows, :]) + (wy[t] + wy_last[t])
                faces = faces + (wz + self.last_deep(wz))
                inv = 1.0 / (MASS + faces)
                flow = (fx - self.flux[rows, :]) + (fy[t] - fy_last[t])
                flow = flow + (fz - self.last_deep(fz))
                residual = self.tile(self.f, x, t) - MASS * u[t] + flow
                q = residual * inv
                p = q * (1.0 / THETA)
                self.flux[rows, :] = fx
                self.wx[x, rows, :] = wx
                self.wy[x, rows, :] = wy[t]
                self.wz[x, rows, :] = wz
                self.inv[x, rows, :] = inv
                self.q[x, rows, :] = q
                self.p[x, rows, :] = p
                self.total[x, rows, :] = u[t] + p
                for j in range(self.lanes):
                    at = pl.ds(t, 8, stride=self.t)
                    self.f[x, j, at, :] = residual[:, 128 * j : 128 * (j + 1)]
            return carry

        lax.fori_loop(1, self.n - 1, body, 0)

    def step(self, level, emit=None):
        keep, gain = step_factors()[level - 1]
        for t in range(self.t):
            rows = self.rows(t)
            change = self.p[level + 1, rows, :] - self.p[level, rows, :]
            self.flux[rows, :] = self.wx[level, rows, :] * change

        def body(x, carry):
            p = [self.p[x, self.rows(t), :] for t in range(self.t)]
            p_row = self.next_row(p)
            fy = [self.wy[x, self.rows(t), :] * (p_row[t] - p[t]) for t in range(self.t)]
            fy_last = self.last_row(fy)
            for t in range(self.t):
                rows = self.rows(t)
                fx = self.wx[x, rows, :] * (self.p[x + 1, rows, :] - p[t])
                fz = self.wz[x, rows, :] * (self.next_deep(p[t]) - p[t])
                flow = (fx - self.flux[rows, :]) + (fy[t] - fy_last[t])
                flow = flow + (fz - self.last_deep(fz))
                self.flux[rows, :] = fx
                q = self.q[x, rows, :] + self.inv[x, rows, :] * (flow - MASS * p[t])
                new = keep * p[t] + gain * q
                total = self.total[x, rows, :] + new
                if emit is None:
                    self.q[x, rows, :] = q
                    self.p[x, rows, :] = new
                    self.total[x, rows, :] = total
                else:
                    for j in range(self.lanes):
                        at = pl.ds(t, 8, stride=self.t)
                        self.plane[j, at, :] = total[:, 128 * j : 128 * (j + 1)]
            if emit is not None:
                own = 8 * (self.t - 1)
                parts = [self.plane[j, 0:own, :] for j in range(self.lanes)]
                emit(x, jnp.concatenate(parts, axis=1))
            return carry

        lax.fori_loop(1 + level, self.n - 1 - level, body, 0)

    def smooth(self, emit):
        self.first_pass()
        for level in range(1, STEPS):
            self.step(level, emit if level == STEPS - 1 else None)


def depth_table(coarse_axis, shape):
    fine_len = shape[1 - coarse_axis]
    fine = lax.broadcasted_iota(jnp.int32, shape, 1 - coarse_axis)
    coarse = lax.broadcasted_iota(jnp.int32, shape, coarse_axis)
    near = (fine == 2 * coarse + 1) | (fine == lax.rem(2 * coarse - 1 + fine_len, fine_len))
    return jnp.where(fine == 2 * coarse, 1.0, jnp.where(near, 0.5, 0.0))


def exact_dot(field, table):
    table = table.astype(jnp.bfloat16)
    head = field.astype(jnp.bfloat16)
    rest = field - head.astype(F32)
    middle = rest.astype(jnp.bfloat16)
    tail = (rest - middle.astype(F32)).astype(jnp.bfloat16)
    parts = [jnp.dot(v, table, preferred_element_type=F32) for v in (head, middle, tail)]
    return (parts[2] + parts[1]) + parts[0]


def restrict_plane(slab, at, before, after, grown, out_ref, row):
    for j in range(4):
        mixed = 0.5 * slab.f[at, j] + 0.25 * (slab.f[before, j] + slab.f[after, j])
        grown[j, 0:8, :] = mixed[NF : NF + 8]
        grown[j, 8 : 8 + NF, :] = mixed[0:NF]
        middle = grown[j, pl.ds(8, NC, stride=2), :]
        beside = grown[j, pl.ds(9, NC, stride=2), :] + grown[j, pl.ds(7, NC, stride=2), :]
        out_ref[pl.ds(row, NC), 128 * j : 128 * (j + 1)] = 0.5 * middle + 0.25 * beside


def lift_plane(deep, row, lifted, at):
    if not isinstance(row, int):
        row = pl.multiple_of(row, 8)
    block = deep[pl.ds(row, 24), :]
    here, there = block[0:NC], pltpu.roll(block, 23, axis=0)[0:NC]
    between = 0.5 * (here + there)
    for j in range(4):
        lanes = slice(128 * j, 128 * (j + 1))
        lifted[at, j, pl.ds(0, NC, stride=2), :] = here[:, lanes]
        lifted[at, j, pl.ds(1, NC, stride=2), :] = between[:, lanes]


def lifted_plane(lifted, low, high):
    parts = [0.5 * (lifted[low, j] + lifted[high, j]) for j in range(4)]
    return jnp.concatenate(parts, axis=1)


def coarse_halo(y_up, y_dn, base, h):
    row = base + 8 * (h // 2)
    lanes = slice(ZC * (h % 2), ZC * (h % 2 + 1))
    return y_up[row : row + 8, lanes], y_dn[row : row + 8, lanes]


def inner_kernel(u, c, f, e, y_up, y_dn, out, out_r, *scratch):
    sems, grown, mixed, deep, lifted = scratch[:5]
    slab = Slab(NF, TF, ZF, 1.0, scratch[5:])
    copies = []
    for a, (source, target) in enumerate(((u, slab.u), (c, slab.c), (f, slab.f))):
        for j in range(4):
            copies.append(
                pltpu.make_async_copy(
                    source.at[:, :, pl.ds(128 * j, 128)],
                    target.at[:, j, pl.ds(0, NF), :],
                    sems.at[a, j],
                )
            )
    for copy in copies:
        copy.start()

    pieces = []
    for i in range(NC):
        up, down = coarse_halo(y_up, y_dn, 8 * (NF + NF // 2), i)
        pieces += [e[i], halo_first(up, down)]
    deep[...] = exact_dot(jnp.concatenate(pieces, 0), depth_table(0, (ZC, ZF)))

    def raise_one(i, carry):
        lift_plane(deep, 24 * i, lifted, i)
        return carry

    lax.fori_loop(2, NC - 1, raise_one, 0)
    for copy in copies:
        copy.wait()

    def fill(m, carry):
        for half in range(2):
            x = 2 * m + half
            row = pl.multiple_of(8 * x, 8)
            up, down = y_up[pl.ds(row, 8), :], y_dn[pl.ds(row, 8), :]
            slab.put_halo(slab.u, x, halo_first(up, down))
            slab.put_halo(slab.c, x, halo_second(up, down))
        row = pl.multiple_of(8 * (NF + m), 8)
        up, down = y_up[pl.ds(row, 8), :], y_dn[pl.ds(row, 8), :]
        slab.put_halo(slab.f, 2 * m, halo_first(up, down))
        slab.put_halo(slab.f, 2 * m + 1, halo_second(up, down))
        return carry

    lax.fori_loop(0, NF // 2, fill, 0)

    def emit(x, own):
        out[x] = own + lifted_plane(lifted, lax.div(x, 2), lax.div(x + 1, 2))

    slab.smooth(emit)

    def lower(i, carry):
        row = pl.multiple_of(NC * (i - 1), 8)
        restrict_plane(slab, 2 * i, 2 * i - 1, 2 * i + 1, grown, mixed, row)
        return carry

    lax.fori_loop(1, NC - 1, lower, 0)
    result = exact_dot(mixed[...], 0.5 * depth_table(1, (ZF, ZC)))
    for i in range(1, NC - 1):
        out_r[i] = result[NC * (i - 1) : NC * i]


def inner(u, c, f, e, y_up, y_dn):
    anywhere = pl.BlockSpec(memory_space=pl.ANY)
    vmem = pl.BlockSpec(memory_space=pltpu.VMEM)
    return pl.pallas_call(
        inner_kernel,
        in_specs=[anywhere] * 3 + [vmem] * 3,
        out_specs=[vmem, vmem],
        out_shape=[
            jax.ShapeDtypeStruct((NF, NF, ZF), F32),
            jax.ShapeDtypeStruct((NC, NC, ZC), F32),
        ],
        scratch_shapes=[
            pltpu.SemaphoreType.DMA((3, 4)),
            pltpu.VMEM((4, NF + 8, 128), F32),
            pltpu.VMEM((NC * (NC - 2), ZF), F32),
            pltpu.VMEM((24 * NC, ZF), F32),
            pltpu.VMEM((NC, 4, NF, 128), F32),
        ]
        + Slab.scratch(NF, TF, ZF),
        compiler_params=pltpu.CompilerParams(vmem_limit_bytes=LIMIT),
        cost_estimate=pl.CostEstimate(
            flops=30_000_000_000, bytes_accessed=12_000_000, transcendentals=0
        ),
        name="inner_planes",
    )(u, c, f, e, y_up, y_dn)


WIDE = 12


def outer_kernel(
    u, c, f, e, cc, cs, y_up, y_dn, x_lo, x_hi, k_lo, k_hi, mid, mid_r,
    out, out_r, out_c, *scratch,
):
    sems, out_sems, grown, mixed, deep, lifted, edge, edge_r = scratch[:8]
    slabs = [Slab(WIDE, TF, ZF, 1.0, scratch[8 + 12 * i : 20 + 12 * i]) for i in range(2)]
    coarse = Slab(NC + 8, TC, ZC, 0.25, scratch[32:44])
    copies = [[], []]
    for side in range(2):
        slab = slabs[side]
        for a, (source, target) in enumerate(((u, slab.u), (c, slab.c), (f, slab.f))):
            for j in range(4):
                copies[side].append(
                    pltpu.make_async_copy(
                        source.at[pl.ds(24 * side, 8), :, pl.ds(128 * j, 128)],
                        target.at[pl.ds(4 * (1 - side), 8), j, pl.ds(0, NF), :],
                        sems.at[side, a, j],
                    )
                )
    for copy in copies[0] + copies[1]:
        copy.start()

    base = 8 * (NF + NF // 2)
    for x in range(NC):
        for target, source in ((coarse.u, e), (coarse.c, cc), (coarse.f, cs)):
            coarse.put_own(target, x + 4, source[x])
        pair = coarse_halo(y_up, y_dn, base, x)
        coarse.put_halo(coarse.u, x + 4, halo_first(*pair))
        coarse.put_halo(coarse.c, x + 4, halo_second(*pair))
        pair = coarse_halo(y_up, y_dn, base, NC + x // 2)
        choose = halo_second if x % 2 else halo_first
        coarse.put_halo(coarse.f, x + 4, choose(*pair))
    for side, faces, corner in ((0, x_lo, k_lo), (1, x_hi, k_hi)):
        slab = slabs[side]
        k = 0
        for which, count in ((0, 4), (1, 4), (2, 3)):
            fine_ref = (slab.u, slab.c, slab.f)[which]
            coarse_ref = (coarse.u, coarse.c, coarse.f)[which]
            for m in range(count):
                dist = count - m
                at = 4 - dist if side == 0 else 7 + dist
                fine_ref_rows = faces[NF * k : NF * (k + 1), :]
                slab.put_own(fine_ref, at, fine_ref_rows)
                row = 11 * NF + 8 * k
                at_c = 4 - dist if side == 0 else 3 + NC + dist
                halves = [faces[row : row + 8, ZC * h : ZC * (h + 1)] for h in range(2)]
                coarse.put_own(coarse_ref, at_c, jnp.concatenate(halves, 0))
                k += 1
                if dist == 4 or (which == 2 and dist == 3):
                    fine_ref[at, :, NF : NF + 8, :] = jnp.zeros((4, 8, 128), F32)
                    coarse_ref[at_c, :, NC : NC + 8, :] = jnp.zeros((2, 8, 128), F32)
                    continue
                if which < 2:
                    near = dist - 1 if side == 1 else 3 - dist
                    up, down = 8 * near, 8 * (3 + near)
                    choose = halo_first if which == 0 else halo_second
                    h = dist - 1 if side == 1 else 4 - dist
                    up_c, down_c = 64 + 8 * (h // 2), 88 + 8 * (h // 2)
                    lanes_c = slice(ZC * (h % 2), ZC * (h % 2 + 1))
                else:
                    plane = dist - 1 if side == 1 else 2 - dist
                    up, down = 48, 56
                    choose = halo_second if plane else halo_first
                    up_c, down_c = 80, 104
                    half = 0 if side == 1 else 1
                    lanes_c = slice(ZC * half, ZC * (half + 1))
                block = choose(corner[up : up + 8, :], corner[down : down + 8, :])
                slab.put_halo(fine_ref, at, block)
                block = choose(corner[up_c : up_c + 8, lanes_c], corner[down_c : down_c + 8, lanes_c])
                coarse.put_halo(coarse_ref, at_c, block)

    pieces = []
    for x in (0, 1, 2, 14, 15, 16):
        pieces.append(jnp.concatenate([coarse.u[x + 4, j] for j in range(2)], axis=1))
    deep[...] = exact_dot(jnp.concatenate(pieces, 0), depth_table(0, (ZC, ZF)))
    for i in range(6):
        lift_plane(deep, 24 * i, lifted, i)

    def emit_coarse(x, own):
        out_c[x - 4] = own

    coarse.smooth(emit_coarse)

    finish = []
    for side in range(2):
        slab = slabs[side]
        for copy in copies[side]:
            copy.wait()
        for i in range(8):
            x = 24 * side + i
            at = i + 4 * (1 - side)
            pair = (y_up[8 * x : 8 * x + 8, :], y_dn[8 * x : 8 * x + 8, :])
            slab.put_halo(slab.u, at, halo_first(*pair))
            slab.put_halo(slab.c, at, halo_second(*pair))
            row = 8 * (NF + x // 2)
            pair = (y_up[row : row + 8, :], y_dn[row : row + 8, :])
            slab.put_halo(slab.f, at, (halo_second if x % 2 else halo_first)(*pair))

        def emit(x, own, side=side):
            low = 3 * side + lax.div(x - 4, 2)
            high = 3 * side + lax.div(x - 3, 2)
            edge[side, x - 4] = own + lifted_plane(lifted, low, high)

        slab.smooth(emit)
        at = 4 if side == 0 else 6
        restrict_plane(slab, at, at - 1, at + 1, grown, mixed, NC * side)
        finish.append(
            pltpu.make_async_copy(
                edge.at[side], out.at[pl.ds((NF - 4) * side, 4)], out_sems.at[side]
            )
        )
        finish[-1].start()

    result = exact_dot(mixed[...], 0.5 * depth_table(1, (ZF, ZC)))
    for side in range(2):
        edge_r[side, 0] = result[NC * side : NC * (side + 1)]
        finish.append(
            pltpu.make_async_copy(
                edge_r.at[side], out_r.at[pl.ds((NC - 1) * side, 1)], out_sems.at[2 + side]
            )
        )
        finish[-1].start()
    for copy in finish:
        copy.wait()


def outer(u, c, f, e, cc, cs, y_up, y_dn, x_lo, x_hi, k_lo, k_hi, mid, mid_r):
    anywhere = pl.BlockSpec(memory_space=pl.ANY)
    vmem = pl.BlockSpec(memory_space=pltpu.VMEM)
    return pl.pallas_call(
        outer_kernel,
        in_specs=[anywhere] * 3 + [vmem] * 9 + [anywhere] * 2,
        out_specs=[anywhere, anywhere, vmem],
        out_shape=[
            jax.ShapeDtypeStruct((NF, NF, ZF), F32),
            jax.ShapeDtypeStruct((NC, NC, ZC), F32),
            jax.ShapeDtypeStruct((NC, NC, ZC), F32),
        ],
        scratch_shapes=[
            pltpu.SemaphoreType.DMA((2, 3, 4)),
            pltpu.SemaphoreType.DMA((4,)),
            pltpu.VMEM((4, NF + 8, 128), F32),
            pltpu.VMEM((2 * NC, ZF), F32),
            pltpu.VMEM((24 * 6, ZF), F32),
            pltpu.VMEM((6, 4, NF, 128), F32),
            pltpu.VMEM((2, 4, NF, ZF), F32),
            pltpu.VMEM((2, 1, NC, ZC), F32),
        ]
        + Slab.scratch(WIDE, TF, ZF) * 2
        + Slab.scratch(NC + 8, TC, ZC),
        compiler_params=pltpu.CompilerParams(vmem_limit_bytes=LIMIT),
        input_output_aliases={12: 0, 13: 1},
        name="outer_planes",
    )(u, c, f, e, cc, cs, y_up, y_dn, x_lo, x_hi, k_lo, k_hi, mid, mid_r)


def shift(block, axis, by):
    count = lax.axis_size(axis)
    return lax.ppermute(block, axis, [(i, (i + by) % count) for i in range(count)])


def relay(y_up, y_dn, side):
    spans = (((0, 3), (32, 33), (48, 50), (56, 57)), ((29, 32), (47, 48), (54, 56), (59, 60)))[side]
    pieces = []
    for group in ((0,), (1,), (2, 3)):
        for ref in (y_up, y_dn):
            for member in group:
                a, b = spans[member]
                pieces.append(ref[8 * a : 8 * b])
    return jnp.concatenate(pieces, 0)


def local(u, f, c, e, cs, cc):
    x_lo, x_hi, y_up, y_dn = pack(u, c, f, e, cc, cs)
    y_up = shift(y_up, "gy", -1)
    y_dn = shift(y_dn, "gy", 1)
    from_hi = shift(x_lo, "gx", -1)
    from_lo = shift(x_hi, "gx", 1)
    corner_hi = shift(relay(y_up, y_dn, 0), "gx", -1)
    corner_lo = shift(relay(y_up, y_dn, 1), "gx", 1)
    mid, mid_r = inner(u, c, f, e, y_up, y_dn)
    return tuple(
        outer(u, c, f, e, cc, cs, y_up, y_dn, from_lo, from_hi, corner_lo, corner_hi, mid, mid_r)
    )


def solution(mesh):
    placed = P("gx", "gy", None)
    return jax.shard_map(
        local,
        mesh=mesh,
        in_specs=(placed,) * 6,
        out_specs=(placed,) * 3,
        check_vma=False,
    )
```

profile of v0, /device:TPU:1, one launch (start us, length us, event | category | flops | bytes accessed | tf_op | source)
XLA Modules:
  0.0 116.1 jit_solution(6926703678266417319)
XLA Ops:
  0.6 4.5 %pack_faces.1 = (f32[440,512]{1,0:T(8,128)}, f32[440,512]{1,0:T(8,128)}, f32[480,512]{1,0:T(8,128)}, f32[480,512]{1,0:T(8,128)}) custom-call(f32[32,32,512]{2,1,0:T(8,128)} %u.3, f32[32,32,512]{2,1,0:T(8,128)} %u.3, f32[32,32,512]{2,1,0:T(8,128)} %c.3, f32[32,32,512]{2,1,0:T(8,128)} %c.3, f32[32,32,512]{2,1,0:T(8,128)} %f.3, f32[32,32,512]{2,1,0:T(8,128)} %f.3, ...), custom_call_target="tpu_custom_call" | custom-call | tf_op jit(solution)/shard_map/pack_faces/pallas_call | solution.py:107
  5.1 3.2 %collective-permute-start = (f32[480,512]{1,0:T(8,128)}, f32[480,512]{1,0:T(8,128)S(1)}, u32[]{:S(2)}, u32[]{:S(2)}) collective-permute-start(f32[480,512]{1,0:T(8,128)} %get-tuple-element.9), channel_id=1, source_target_pairs={{0,15},{1,0},{2,1},{3,2},{4,3},{5,4},{6,5},{7,6},{8,7},{9,8},{10,9... | collective-permute-start | bytes 2949128 | tf_op jit(solution)/shard_map/ppermute | solution.py:558
  8.4 0.0 collective-permute-start.1
  8.4 1.2 %collective-permute-start.2 = (f32[440,512]{1,0:T(8,128)}, f32[440,512]{1,0:T(8,128)S(1)}, u32[]{:S(2)}, u32[]{:S(2)}) collective-permute-start(f32[440,512]{1,0:T(8,128)} %get-tuple-element.11), channel_id=1, source_target_pairs={{0,16},{16,32},{32,48},{48,64},{64,80},{80,96},{96,112},{112,128},... | collective-permute-start | bytes 2703368 | tf_op jit(solution)/shard_map/ppermute | solution.py:558
  9.5 6.4 %collective-permute-start.3 = (f32[440,512]{1,0:T(8,128)}, f32[440,512]{1,0:T(8,128)S(1)}, u32[]{:S(2)}, u32[]{:S(2)}) collective-permute-start(f32[440,512]{1,0:T(8,128)} %get-tuple-element.12), channel_id=1, source_target_pairs={{0,240},{16,0},{32,16},{48,32},{64,48},{80,64},{96,80},{112,96},{1... | collective-permute-start | bytes 2703368 | tf_op jit(solution)/shard_map/ppermute | solution.py:558
  15.9 36.5 %collective-permute-done.y_up = f32[480,512]{1,0:T(8,128)S(1)} collective-permute-done((f32[480,512]{1,0:T(8,128)}, f32[480,512]{1,0:T(8,128)S(1)}, u32[]{:S(2)}, u32[]{:S(2)}) %collective-permute-start) | collective-permute-done | bytes 983072 | tf_op jit(solution)/shard_map/ppermute | solution.py:558
  52.4 0.0 copy-start
  52.4 0.0 collective-permute-done.1.y_dn
  52.4 0.0 copy-start.1
  52.5 7.9 %collective-permute-start.5 = (f32[112,512]{1,0:T(8,128)S(1)}, f32[112,512]{1,0:T(8,128)S(1)}, u32[]{:S(2)}, u32[]{:S(2)}) collective-permute-start(f32[112,512]{1,0:T(8,128)S(1)} %get-tuple-element.15), channel_id=1, source_target_pairs={{0,240},{16,0},{32,16},{48,32},{64,48},{80,64},{96,80},{112,96},{1... | collective-permute-start | bytes 688136 | tf_op jit(solution)/shard_map/ppermute | solution.py:558
  60.4 0.0 collective-permute-start.4
  60.4 0.0 copy-done
  60.4 0.0 copy-done.1
  60.4 26.5 %inner_planes.1 = (f32[32,32,512]{2,1,0:T(8,128)}, f32[16,16,256]{2,1,0:T(8,128)}) custom-call(f32[32,32,512]{2,1,0:T(8,128)} %u.3, f32[32,32,512]{2,1,0:T(8,128)} %c.3, f32[32,32,512]{2,1,0:T(8,128)} %f.3, f32[16,16,256]{2,1,0:T(8,128)} %e.5, f32[480,512]{1,0:T(8,128)} %copy-done, f32[480,512]{1,0:T(8,128)} %copy-done.1), custom_call_target="tpu_custom_call" | custom-call | flops 30000001024 | bytes 12000000 | tf_op jit(solution)/shard_map/inner_planes/pallas_call | solution.py:373
  87.0 0.0 collective-permute-done.2.x_lo
  87.0 0.0 copy-start.2
  87.0 0.0 collective-permute-done.3.x_hi
  87.0 0.0 copy-start.3
  87.0 0.0 collective-permute-done.5.k_hi
  87.0 0.0 copy-start.4
  87.0 0.0 collective-permute-done.4.k_lo
  87.0 0.0 copy-start.5
  87.0 0.9 copy-done.2
  87.9 0.3 copy-done.3
  88.2 0.1 copy-done.4
  88.2 0.1 copy-done.5
  88.3 27.8 %outer_planes.1 = (f32[32,32,512]{2,1,0:T(8,128)}, f32[16,16,256]{2,1,0:T(8,128)}, f32[16,16,256]{2,1,0:T(8,128)}) custom-call(f32[32,32,512]{2,1,0:T(8,128)} %u.3, f32[32,32,512]{2,1,0:T(8,128)} %c.3, f32[32,32,512]{2,1,0:T(8,128)} %f.3, f32[16,16,256]{2,1,0:T(8,128)} %e.5, f32[16,16,256]{2,1,0:T(8,128)} %cc.3, ...), custom_call_target="tpu_custom_call", output_to_operand_aliasing={{0}: (12, {}), {1}: (13, {})} | custom-call | tf_op jit(solution)/shard_map/outer_planes/pallas_call | solution.py:529
  (8 shorter events, 0.1 us)
Async XLA Ops:
  5.1 47.3 %collective-permute-start = (f32[480,512]{1,0:T(8,128)}, f32[480,512]{1,0:T(8,128)S(1)}, u32[]{:S(2)}, u32[]{:S(2)}) collective-permute-start(f32[480,512]{1,0:T(8,128)} %get-tuple-element.9), channel_id=1, source_target_pairs={{0,15},{1,0},{2,1},{3,2},{4,3},{5,4},{6,5},{7,6},{8,7},{9,8},{10,9... | collective-permute-start | bytes 2949128 | tf_op jit(solution)/shard_map/ppermute | solution.py:558
  8.4 44.0 %collective-permute-start.1 = (f32[480,512]{1,0:T(8,128)}, f32[480,512]{1,0:T(8,128)S(1)}, u32[]{:S(2)}, u32[]{:S(2)}) collective-permute-start(f32[480,512]{1,0:T(8,128)} %get-tuple-element.10), channel_id=1, source_target_pairs={{0,1},{1,2},{2,3},{3,4},{4,5},{5,6},{6,7},{7,8},{8,9},{9,10},{10,1... | collective-permute-start | bytes 2949128 | tf_op jit(solution)/shard_map/ppermute | solution.py:558
  8.4 78.6 %collective-permute-start.2 = (f32[440,512]{1,0:T(8,128)}, f32[440,512]{1,0:T(8,128)S(1)}, u32[]{:S(2)}, u32[]{:S(2)}) collective-permute-start(f32[440,512]{1,0:T(8,128)} %get-tuple-element.11), channel_id=1, source_target_pairs={{0,16},{16,32},{32,48},{48,64},{64,80},{80,96},{96,112},{112,128},... | collective-permute-start | bytes 2703368 | tf_op jit(solution)/shard_map/ppermute | solution.py:558
  9.5 77.4 %collective-permute-start.3 = (f32[440,512]{1,0:T(8,128)}, f32[440,512]{1,0:T(8,128)S(1)}, u32[]{:S(2)}, u32[]{:S(2)}) collective-permute-start(f32[440,512]{1,0:T(8,128)} %get-tuple-element.12), channel_id=1, source_target_pairs={{0,240},{16,0},{32,16},{48,32},{64,48},{80,64},{96,80},{112,96},{1... | collective-permute-start | bytes 2703368 | tf_op jit(solution)/shard_map/ppermute | solution.py:558
  52.4 8.0 %copy-start = (f32[480,512]{1,0:T(8,128)}, f32[480,512]{1,0:T(8,128)S(1)}, u32[]{:S(2)}) copy-start(f32[480,512]{1,0:T(8,128)S(1)} %collective-permute-done.y_up) | copy-start | bytes 2949124
  52.4 8.0 %copy-start.1 = (f32[480,512]{1,0:T(8,128)}, f32[480,512]{1,0:T(8,128)S(1)}, u32[]{:S(2)}) copy-start(f32[480,512]{1,0:T(8,128)S(1)} %collective-permute-done.1.y_dn) | copy-start | bytes 2949124
  52.5 34.5 %collective-permute-start.5 = (f32[112,512]{1,0:T(8,128)S(1)}, f32[112,512]{1,0:T(8,128)S(1)}, u32[]{:S(2)}, u32[]{:S(2)}) collective-permute-start(f32[112,512]{1,0:T(8,128)S(1)} %get-tuple-element.15), channel_id=1, source_target_pairs={{0,240},{16,0},{32,16},{48,32},{64,48},{80,64},{96,80},{112,96},{1... | collective-permute-start | bytes 688136 | tf_op jit(solution)/shard_map/ppermute | solution.py:558
  60.4 26.6 %collective-permute-start.4 = (f32[112,512]{1,0:T(8,128)S(1)}, f32[112,512]{1,0:T(8,128)S(1)}, u32[]{:S(2)}, u32[]{:S(2)}) collective-permute-start(f32[112,512]{1,0:T(8,128)S(1)} %get-tuple-element.16), channel_id=1, source_target_pairs={{0,16},{16,32},{32,48},{48,64},{64,80},{80,96},{96,112},{112,128},... | collective-permute-start | bytes 688136 | tf_op jit(solution)/shard_map/ppermute | solution.py:558
  87.0 0.9 copy-start.2
  87.0 1.2 %copy-start.3 = (f32[440,512]{1,0:T(8,128)}, f32[440,512]{1,0:T(8,128)S(1)}, u32[]{:S(2)}) copy-start(f32[440,512]{1,0:T(8,128)S(1)} %collective-permute-done.3.x_hi) | copy-start | bytes 2703364
  87.0 1.2 %copy-start.4 = (f32[112,512]{1,0:T(8,128)}, f32[112,512]{1,0:T(8,128)S(1)}, u32[]{:S(2)}) copy-start(f32[112,512]{1,0:T(8,128)S(1)} %collective-permute-done.5.k_hi) | copy-start | bytes 688132
  87.0 1.3 %copy-start.5 = (f32[112,512]{1,0:T(8,128)}, f32[112,512]{1,0:T(8,128)S(1)}, u32[]{:S(2)}) copy-start(f32[112,512]{1,0:T(8,128)S(1)} %collective-permute-done.4.k_lo) | copy-start | bytes 688132
where the time goes:
time: 116 us
  Pallas kernels  58.8 us (51%)
  waiting for transfers between devices  36.5 us (31%)
  starting transfers between devices  18.7 us (16%)
  local copies, waits for them, and re-layouts  1.34 us (1%)
    ppermute x6, waiting for transfers between devices, shift(): lax.ppermute(block, axis, [(i, (i + by) % count) for i in range(count)])  36.5 us
    pallas_call x1, Pallas kernels, outer(): pl.pallas_call(outer_kernel, in_specs=[anywhere] * 3 + [vmem] * 9 + [anyw...  27.8 us
    pallas_call x1, Pallas kernels, inner(): pl.pallas_call(inner_kernel, in_specs=[anywhere] * 3 + [vmem] * 3, out_sp...  26.5 us
    ppermute x6, starting transfers between devices, shift(): lax.ppermute(block, axis, [(i, (i + by) % count) for i in range(count)])  18.7 us
    pallas_call x1, Pallas kernels, pack(): pl.pallas_call(pack_kernel, grid=(1,), in_specs=[face(0), face(1)] * 3 +...  4.5 us
  transfers between devices with their start and end apart: 6, of which 1 were waited for; matrix products, arithmetic and copies ran while one was open for 0% of the time, Pallas kernels for 23%

commit v1 on v0

v1 whole, which is shorter than its diff:
```python
import jax
import jax.numpy as jnp
from jax import lax
from jax.experimental import pallas as pl
from jax.experimental.pallas import tpu as pltpu
from jax.sharding import PartitionSpec as P

MASS = 0.2
THETA = 1.125
DELTA = 0.875
SIGMA = THETA / DELTA
STEPS = 4
F32 = jnp.float32

NF, ZF, TF = 32, 512, 5
NC, ZC, TC = 16, 256, 3
XROWS = 7 * 8 * TF + 4 * 8 * TC
YROWS = 8 * (NF + NF // 2 + 12)
LIMIT = 56 * 1024 * 1024


def step_factors():
    ratio = 1.0 / SIGMA
    factors = []
    for _ in range(STEPS - 1):
        following = 1.0 / (2.0 * SIGMA - ratio)
        factors.append((following * ratio, 2.0 * following / DELTA))
        ratio = following
    return factors


def upper_rows(shape):
    return lax.broadcasted_iota(jnp.int32, shape, len(shape) - 2) < 4


def turn(block):
    return pltpu.roll(block, 4, axis=block.ndim - 2)


def pair_up(first, second):
    return jnp.where(upper_rows(first.shape), first, turn(second))


def pair_down(first, second):
    return jnp.where(upper_rows(first.shape), turn(second), first)


def halo_first(up, down):
    return jnp.where(upper_rows(up.shape), up, down)


def halo_second(up, down):
    return turn(jnp.where(upper_rows(up.shape), down, up))


def pack_y_kernel(u_r0, u_r3, c_r0, c_r3, f_r0, f_r3, e, cc, cs, y_up, y_dn):
    for x in range(NF):
        y_up[8 * x : 8 * x + 8, :] = pair_up(u_r0[x], c_r0[x])
        y_dn[8 * x : 8 * x + 8, :] = pair_down(u_r3[x], c_r3[x])
    for m in range(NF // 2):
        row = 8 * (NF + m)
        y_up[row : row + 8, :] = pair_up(f_r0[2 * m], f_r0[2 * m + 1])
        y_dn[row : row + 8, :] = pair_down(f_r3[2 * m], f_r3[2 * m + 1])
    for h in range(NC + NC // 2):
        row = 8 * (NF + NF // 2 + h // 2)
        lanes = slice(ZC * (h % 2), ZC * (h % 2 + 1))
        if h < NC:
            pair = ((e, h), (cc, h))
        else:
            pair = ((cs, 2 * (h - NC)), (cs, 2 * (h - NC) + 1))
        low = [ref[i, 0:8, :] for ref, i in pair]
        high = [ref[i, 8:16, :] for ref, i in pair]
        y_up[row : row + 8, lanes] = pair_up(*low)
        y_dn[row : row + 8, lanes] = pair_down(*high)


def pack_y(u, c, f, e, cc, cs):
    def strip(at):
        return pl.BlockSpec((NF, 8, ZF), lambda i: (0, at, 0))

    whole = pl.BlockSpec((NC, NC, ZC), lambda i: (0, 0, 0))
    y_spec = pl.BlockSpec((YROWS, ZF), lambda i: (0, 0))
    return pl.pallas_call(
        pack_y_kernel,
        grid=(1,),
        in_specs=[strip(0), strip(3)] * 3 + [whole] * 3,
        out_specs=[y_spec, y_spec],
        out_shape=[jax.ShapeDtypeStruct((YROWS, ZF), F32)] * 2,
        compiler_params=pltpu.CompilerParams(vmem_limit_bytes=LIMIT),
        name="pack_gy_faces",
    )(u, u, c, c, f, f, e, cc, cs)


class Slab:
    def __init__(self, own, tiles, depth, scale, natural, work, shift=0, flipped=False):
        self.own, self.t, self.z, self.scale = own, tiles, depth, scale
        self.lanes, self.shift, self.flipped = depth // 128, shift, flipped
        self.u, self.c, self.f = natural
        if work:
            (
                self.p, self.q, self.total, self.wx, self.wy, self.wz, self.wz_last,
                self.inv, self.flux, self.plane,
            ) = work

    @staticmethod
    def natural(planes, tiles, depth):
        return [pltpu.VMEM((planes, depth // 128, 8 * tiles, 128), F32)] * 3

    @staticmethod
    def work(planes, tiles, depth):
        rows, lanes = 8 * tiles, depth // 128
        return [pltpu.VMEM((planes, rows, depth), F32)] * 8 + [
            pltpu.VMEM((rows, depth), F32),
            pltpu.VMEM((lanes, rows, 128), F32),
        ]

    def at(self, x):
        return self.own - 1 - (x - self.shift) if self.flipped else x - self.shift

    def tile(self, ref, x, t):
        x = self.at(x)
        parts = [ref[x, j, pl.ds(t, 8, stride=self.t), :] for j in range(self.lanes)]
        return jnp.concatenate(parts, axis=1)

    def tiles(self, ref, x):
        return [self.tile(ref, x, t) for t in range(self.t)]

    def put_tile(self, ref, index, t, value):
        for j in range(self.lanes):
            ref[index, j, pl.ds(t, 8, stride=self.t), :] = value[:, 128 * j : 128 * (j + 1)]

    def rows(self, t):
        return slice(8 * t, 8 * t + 8)

    def put_halo(self, ref, index, block):
        top = 8 * (self.t - 1)
        for j in range(self.lanes):
            ref[index, j, top : top + 8, :] = block[:, 128 * j : 128 * (j + 1)]

    def put_own(self, ref, index, block):
        own = 8 * (self.t - 1)
        for j in range(self.lanes):
            ref[index, j, 0:own, :] = block[:, 128 * j : 128 * (j + 1)]

    def next_row(self, values):
        return values[1:] + [pltpu.roll(values[0], 7, axis=0)]

    def last_row(self, values):
        return [pltpu.roll(values[-1], 1, axis=0)] + values[:-1]

    def next_deep(self, value):
        return pltpu.roll(value, self.z - 1, axis=1)

    def last_deep(self, value):
        return pltpu.roll(value, 1, axis=1)

    def cross_weights(self, c):
        half = 0.5 * self.scale
        ahead, behind = self.next_row(c), self.last_row(c)
        wy = [half * (c[t] + ahead[t]) for t in range(self.t)]
        wy_last = [half * (c[0] + behind[0])] + wy[:-1]
        wz = [half * (v + self.next_deep(v)) for v in c]
        wz_last = [half * (v + self.last_deep(v)) for v in c]
        return wy, wy_last, wz, wz_last

    def cross_flow(self, v, wy, wy_last, wz, wz_last):
        ahead, behind = self.next_row(v), self.last_row(v)
        fy = [wy[t] * (ahead[t] - v[t]) for t in range(self.t)]
        fy_last = [wy_last[0] * (v[0] - behind[0])] + fy[:-1]
        flow = []
        for t in range(self.t):
            fz = wz[t] * (self.next_deep(v[t]) - v[t])
            fz_last = wz_last[t] * (v[t] - self.last_deep(v[t]))
            flow.append((fy[t] - fy_last[t]) + (fz - fz_last))
        return flow

    def keep_weights(self, x, t, wy, wz, wz_last, faces):
        rows = self.rows(t)
        inv = 1.0 / (MASS + faces)
        self.wy[x, rows, :] = wy
        self.wz[x, rows, :] = wz
        self.wz_last[x, rows, :] = wz_last
        self.inv[x, rows, :] = inv
        return inv

    def open_end(self, x):
        u0, u1 = self.tiles(self.u, x), self.tiles(self.u, x + 1)
        c0, c1 = self.tiles(self.c, x), self.tiles(self.c, x + 1)
        for t in range(self.t):
            w = 0.5 * self.scale * (c0[t] + c1[t])
            self.wx[x, self.rows(t), :] = w
            self.flux[self.rows(t), :] = w * (u1[t] - u0[t])

    def halo_end(self, far, read, start):
        half = 0.5 * self.scale
        step = 1 if start else -1
        mid, near, own = far + step, far + 2 * step, far + 3 * step
        message = [[read(k, t) for t in range(self.t)] for k in range(7)]
        u1, c1, c2, c3, r1, p2, p3 = message
        u_own, c_own = self.tiles(self.u, own), self.tiles(self.c, own)
        cross2, cross1 = self.cross_weights(c2), self.cross_weights(c1)
        for t in range(self.t):
            rows = self.rows(t)
            outer, middle, inner = half * (c3[t] + c2[t]), half * (c2[t] + c1[t]), half * (c1[t] + c_own[t])
            self.wx[min(far, mid), rows, :] = outer
            self.wx[min(mid, near), rows, :] = middle
            self.wx[min(near, own), rows, :] = inner
            self.p[far, rows, :] = p3[t]
            wy, wy_last, wz, wz_last = [w[t] for w in cross2]
            faces = (outer + middle) + (wy + wy_last) + (wz + wz_last)
            self.keep_weights(mid, t, wy, wz, wz_last, faces)
            self.p[mid, rows, :] = p2[t]
            self.q[mid, rows, :] = THETA * p2[t]
            wy, wy_last, wz, wz_last = [w[t] for w in cross1]
            faces = (middle + inner) + (wy + wy_last) + (wz + wz_last)
            inv = self.keep_weights(near, t, wy, wz, wz_last, faces)
            flux = inner * (u_own[t] - u1[t])
            residual = r1[t] + flux
            q = residual * inv
            self.q[near, rows, :] = q
            self.p[near, rows, :] = q * (1.0 / THETA)
            if start:
                self.flux[rows, :] = flux
                self.put_tile(self.f, self.own, t, residual)

    def first_plane(self, x):
        half = 0.5 * self.scale
        u, c = self.tiles(self.u, x), self.tiles(self.c, x)
        wy, wy_last, wz, wz_last = self.cross_weights(c)
        cross = self.cross_flow(u, wy, wy_last, wz, wz_last)
        for t in range(self.t):
            rows = self.rows(t)
            wx = half * (c[t] + self.tile(self.c, x + 1, t))
            fx = wx * (self.tile(self.u, x + 1, t) - u[t])
            faces = (wx + self.wx[x - 1, rows, :]) + (wy[t] + wy_last[t]) + (wz[t] + wz_last[t])
            inv = self.keep_weights(x, t, wy[t], wz[t], wz_last[t], faces)
            flow = (fx - self.flux[rows, :]) + cross[t]
            residual = self.tile(self.f, x, t) - MASS * u[t] + flow
            q = residual * inv
            p = q * (1.0 / THETA)
            self.flux[rows, :] = fx
            self.wx[x, rows, :] = wx
            self.q[x, rows, :] = q
            self.p[x, rows, :] = p
            self.total[x, rows, :] = u[t] + p
            self.put_tile(self.f, self.at(x), t, residual)

    def start_step(self, x):
        for t in range(self.t):
            rows = self.rows(t)
            change = self.p[x, rows, :] - self.p[x - 1, rows, :]
            self.flux[rows, :] = self.wx[x - 1, rows, :] * change

    def step_plane(self, level, x, emit):
        keep, gain = step_factors()[level - 1]
        p = [self.p[x, self.rows(t), :] for t in range(self.t)]
        weights = [
            [ref[x, self.rows(t), :] for t in range(self.t)]
            for ref in (self.wy, self.wz, self.wz_last)
        ]
        wy_last = self.last_row(weights[0])
        cross = self.cross_flow(p, weights[0], wy_last, weights[1], weights[2])
        for t in range(self.t):
            rows = self.rows(t)
            fx = self.wx[x, rows, :] * (self.p[x + 1, rows, :] - p[t])
            flow = (fx - self.flux[rows, :]) + cross[t]
            self.flux[rows, :] = fx
            q = self.q[x, rows, :] + self.inv[x, rows, :] * (flow - MASS * p[t])
            new = keep * p[t] + gain * q
            total = self.total[x, rows, :] + new
            if emit is None:
                self.q[x, rows, :] = q
                self.p[x, rows, :] = new
                self.total[x, rows, :] = total
            else:
                for j in range(self.lanes):
                    at = pl.ds(t, 8, stride=self.t)
                    self.plane[j, at, :] = total[:, 128 * j : 128 * (j + 1)]
        if emit is not None:
            own = 8 * (self.t - 1)
            parts = [self.plane[j, 0:own, :] for j in range(self.lanes)]
            emit(x, jnp.concatenate(parts, axis=1))


def sweep(slabs, low, high, act, unroll=2):
    def body(x, carry):
        for slab in slabs:
            act(slab, x)
        return carry

    lax.fori_loop(low, high, body, 0, unroll=unroll)


def smooth(slabs, first, last, low, high, emits, unroll=2):
    sweep(slabs, first, last, lambda slab, x: slab.first_plane(x), unroll)
    for level in range(1, STEPS):
        for slab in slabs:
            slab.start_step(low(level))

        def act(slab, x, level=level):
            emit = emits[slabs.index(slab)] if level == STEPS - 1 else None
            slab.step_plane(level, x, emit)

        sweep(slabs, low(level), high(level), act, unroll)


def depth_table(coarse_axis, shape):
    fine_len = shape[1 - coarse_axis]
    fine = lax.broadcasted_iota(jnp.int32, shape, 1 - coarse_axis)
    coarse = lax.broadcasted_iota(jnp.int32, shape, coarse_axis)
    near = (fine == 2 * coarse + 1) | (fine == lax.rem(2 * coarse - 1 + fine_len, fine_len))
    return jnp.where(fine == 2 * coarse, 1.0, jnp.where(near, 0.5, 0.0))


def exact_dot(field, table):
    table = table.astype(jnp.bfloat16)
    head = field.astype(jnp.bfloat16)
    rest = field - head.astype(F32)
    middle = rest.astype(jnp.bfloat16)
    tail = (rest - middle.astype(F32)).astype(jnp.bfloat16)
    parts = [jnp.dot(v, table, preferred_element_type=F32) for v in (head, middle, tail)]
    return (parts[2] + parts[1]) + parts[0]


def restrict_plane(slab, at, before, after, grown, out_ref, row):
    for j in range(4):
        mixed = 0.5 * slab.f[at, j] + 0.25 * (slab.f[before, j] + slab.f[after, j])
        grown[j, 0:8, :] = mixed[NF : NF + 8]
        grown[j, 8 : 8 + NF, :] = mixed[0:NF]
        middle = grown[j, pl.ds(8, NC, stride=2), :]
        beside = grown[j, pl.ds(9, NC, stride=2), :] + grown[j, pl.ds(7, NC, stride=2), :]
        out_ref[pl.ds(row, NC), 128 * j : 128 * (j + 1)] = 0.5 * middle + 0.25 * beside


def lift_plane(deep, row, lifted, at):
    if not isinstance(row, int):
        row = pl.multiple_of(row, 8)
    block = deep[pl.ds(row, 24), :]
    here, there = block[0:NC], pltpu.roll(block, 23, axis=0)[0:NC]
    between = 0.5 * (here + there)
    for j in range(4):
        lanes = slice(128 * j, 128 * (j + 1))
        lifted[at, j, pl.ds(0, NC, stride=2), :] = here[:, lanes]
        lifted[at, j, pl.ds(1, NC, stride=2), :] = between[:, lanes]


def lifted_plane(lifted, low, high):
    parts = [0.5 * (lifted[low, j] + lifted[high, j]) for j in range(4)]
    return jnp.concatenate(parts, axis=1)


def coarse_halo(y_up, y_dn, base, h):
    row = base + 8 * (h // 2)
    lanes = slice(ZC * (h % 2), ZC * (h % 2 + 1))
    return y_up[row : row + 8, lanes], y_dn[row : row + 8, lanes]


def inner_kernel(u, c, f, e, y_up, y_dn, out, out_r, *scratch):
    sems, grown, mixed, deep, lifted = scratch[:5]
    slab = Slab(NF, TF, ZF, 1.0, scratch[5:8], scratch[8:])
    copies = []
    for a, (source, target) in enumerate(((u, slab.u), (c, slab.c), (f, slab.f))):
        for j in range(4):
            copies.append(
                pltpu.make_async_copy(
                    source.at[:, :, pl.ds(128 * j, 128)],
                    target.at[:, j, pl.ds(0, NF), :],
                    sems.at[a, j],
                )
            )
    for copy in copies:
        copy.start()

    pieces = []
    for i in range(NC):
        up, down = coarse_halo(y_up, y_dn, 8 * (NF + NF // 2), i)
        pieces += [e[i], halo_first(up, down)]
    deep[...] = exact_dot(jnp.concatenate(pieces, 0), depth_table(0, (ZC, ZF)))

    def raise_one(i, carry):
        lift_plane(deep, 24 * i, lifted, i)
        return carry

    lax.fori_loop(2, NC - 1, raise_one, 0)
    for copy in copies:
        copy.wait()

    def fill(m, carry):
        for half in range(2):
            x = 2 * m + half
            row = pl.multiple_of(8 * x, 8)
            up, down = y_up[pl.ds(row, 8), :], y_dn[pl.ds(row, 8), :]
            slab.put_halo(slab.u, x, halo_first(up, down))
            slab.put_halo(slab.c, x, halo_second(up, down))
        row = pl.multiple_of(8 * (NF + m), 8)
        up, down = y_up[pl.ds(row, 8), :], y_dn[pl.ds(row, 8), :]
        slab.put_halo(slab.f, 2 * m, halo_first(up, down))
        slab.put_halo(slab.f, 2 * m + 1, halo_second(up, down))
        return carry

    lax.fori_loop(0, NF // 2, fill, 0)

    def emit(x, own):
        out[x] = own + lifted_plane(lifted, lax.div(x, 2), lax.div(x + 1, 2))

    slab.open_end(0)
    smooth([slab], 1, NF - 1, lambda k: 1 + k, lambda k: NF - 1 - k, [emit])

    def lower(i, carry):
        row = pl.multiple_of(NC * (i - 1), 8)
        restrict_plane(slab, 2 * i, 2 * i - 1, 2 * i + 1, grown, mixed, row)
        return carry

    lax.fori_loop(1, NC - 1, lower, 0)
    result = exact_dot(mixed[...], 0.5 * depth_table(1, (ZF, ZC)))
    for i in range(1, NC - 1):
        out_r[i] = result[NC * (i - 1) : NC * i]


def inner(u, c, f, e, y_up, y_dn):
    anywhere = pl.BlockSpec(memory_space=pl.ANY)
    vmem = pl.BlockSpec(memory_space=pltpu.VMEM)
    return pl.pallas_call(
        inner_kernel,
        in_specs=[anywhere] * 3 + [vmem] * 3,
        out_specs=[vmem, vmem],
        out_shape=[
            jax.ShapeDtypeStruct((NF, NF, ZF), F32),
            jax.ShapeDtypeStruct((NC, NC, ZC), F32),
        ],
        scratch_shapes=[
            pltpu.SemaphoreType.DMA((3, 4)),
            pltpu.VMEM((4, NF + 8, 128), F32),
            pltpu.VMEM((NC * (NC - 2), ZF), F32),
            pltpu.VMEM((24 * NC, ZF), F32),
            pltpu.VMEM((NC, 4, NF, 128), F32),
        ]
        + Slab.natural(NF, TF, ZF)
        + Slab.work(NF, TF, ZF),
        compiler_params=pltpu.CompilerParams(vmem_limit_bytes=LIMIT),
        cost_estimate=pl.CostEstimate(
            flops=30_000_000_000, bytes_accessed=12_000_000, transcendentals=0
        ),
        name="inner_planes",
    )(u, c, f, e, y_up, y_dn)


def first_planes(slab, write):
    half = 0.5 * slab.scale
    u, c = [[slab.tiles(ref, x) for x in range(4)] for ref in (slab.u, slab.c)]
    wx = [[half * (c[x][t] + c[x + 1][t]) for t in range(slab.t)] for x in range(3)]
    fx = [[wx[x][t] * (u[x + 1][t] - u[x][t]) for t in range(slab.t)] for x in range(3)]
    for t in range(slab.t):
        write(0, t, u[0][t])
        for x in range(3):
            write(1 + x, t, c[x][t])
    for x in range(3):
        weights = slab.cross_weights(c[x])
        cross = slab.cross_flow(u[x], *weights)
        for t in range(slab.t):
            part = slab.tile(slab.f, x, t) - MASS * u[x][t] + cross[t] + fx[x][t]
            if x == 0:
                write(4, t, part)
                continue
            wy, wy_last, wz, wz_last = [w[t] for w in weights]
            faces = (wx[x][t] + wx[x - 1][t]) + (wy + wy_last) + (wz + wz_last)
            write(4 + x, t, (part - fx[x - 1][t]) / (MASS + faces) * (1.0 / THETA))


def fine_place(k, t):
    row = 8 * TF * k + 8 * t
    return slice(row, row + 8), slice(0, ZF)


def coarse_place(k, t):
    row = 7 * 8 * TF + 8 * TC * (k // 2) + 8 * t
    return slice(row, row + 8), slice(ZC * (k % 2), ZC * (k % 2 + 1))


def fill_fine(slab, refs, blocks, first, planes):
    y_up, y_dn = refs
    for i in range(planes):
        x = first + i
        if blocks is not None:
            for target, block in zip((slab.u, slab.c, slab.f), blocks):
                slab.put_own(target, i, block[i])
        pair = (y_up[8 * x : 8 * x + 8, :], y_dn[8 * x : 8 * x + 8, :])
        slab.put_halo(slab.u, i, halo_first(*pair))
        slab.put_halo(slab.c, i, halo_second(*pair))
        row = 8 * (NF + x // 2)
        pair = (y_up[row : row + 8, :], y_dn[row : row + 8, :])
        slab.put_halo(slab.f, i, (halo_second if x % 2 else halo_first)(*pair))


def fill_coarse(slab, refs, fields, planes):
    base = 8 * (NF + NF // 2)
    for x, place in planes:
        for target, source in zip((slab.u, slab.c, slab.f), fields):
            slab.put_own(target, place, source[x])
        pair = coarse_halo(*refs, base, x)
        slab.put_halo(slab.u, place, halo_first(*pair))
        slab.put_halo(slab.c, place, halo_second(*pair))
        pair = coarse_halo(*refs, base, NC + x // 2)
        slab.put_halo(slab.f, place, (halo_second if x % 2 else halo_first)(*pair))


def pack_x_kernel(
    u_lo, u_hi, c_lo, c_hi, f_lo, f_hi, e, cc, cs, y_up, y_dn, x_lo, x_hi, *scratch
):
    for side, blocks, out in ((0, (u_lo, c_lo, f_lo), x_lo), (1, (u_hi, c_hi, f_hi), x_hi)):
        slab = Slab(4, TF, ZF, 1.0, scratch[6 * side : 6 * side + 3], (), 0, side == 1)
        fill_fine(slab, (y_up, y_dn), blocks, 28 * side, 4)

        def write_fine(k, t, value, out=out):
            out[fine_place(k, t)] = value

        first_planes(slab, write_fine)
        slab = Slab(4, TC, ZC, 0.25, scratch[6 * side + 3 : 6 * side + 6], (), 0, side == 1)
        fill_coarse(slab, (y_up, y_dn), (e, cc, cs), [(12 * side + i, i) for i in range(4)])

        def write_coarse(k, t, value, out=out):
            out[coarse_place(k, t)] = value

        first_planes(slab, write_coarse)
        for t in range(TC):
            out[coarse_place(7, t)] = jnp.zeros((8, ZC), F32)


def pack_x(u, c, f, e, cc, cs, y_up, y_dn):
    def face(side):
        return pl.BlockSpec((4, NF, ZF), lambda i: (7 * side, 0, 0))

    whole = pl.BlockSpec((NC, NC, ZC), lambda i: (0, 0, 0))
    y_spec = pl.BlockSpec((YROWS, ZF), lambda i: (0, 0))
    x_spec = pl.BlockSpec((XROWS, ZF), lambda i: (0, 0))
    return pl.pallas_call(
        pack_x_kernel,
        grid=(1,),
        in_specs=[face(0), face(1)] * 3 + [whole] * 3 + [y_spec] * 2,
        out_specs=[x_spec, x_spec],
        out_shape=[jax.ShapeDtypeStruct((XROWS, ZF), F32)] * 2,
        scratch_shapes=(Slab.natural(4, TF, ZF) + Slab.natural(4, TC, ZC)) * 2,
        compiler_params=pltpu.CompilerParams(vmem_limit_bytes=LIMIT),
        name="pack_gx_faces",
    )(u, u, c, c, f, f, e, cc, cs, y_up, y_dn)


WIDE = 8


def outer_kernel(
    u, c, f, e, cc, cs, y_up, y_dn, x_lo, x_hi, mid, mid_r, out, out_r, out_c, *scratch
):
    sems, out_sems, grown, mixed, deep, lifted, edge, edge_r = scratch[:8]
    slabs = []
    for side in range(2):
        refs = scratch[8 + 13 * side : 21 + 13 * side]
        slabs.append(Slab(WIDE, TF, ZF, 1.0, refs[:3], refs[3:], 3, side == 1))
    coarse = Slab(NC, TC, ZC, 0.25, scratch[34:37], scratch[37:47], 3)
    copies = []
    for side in range(2):
        slab = slabs[side]
        for a, (source, target) in enumerate(((u, slab.u), (c, slab.c), (f, slab.f))):
            for j in range(4):
                copies.append(
                    pltpu.make_async_copy(
                        source.at[pl.ds((NF - WIDE) * side, WIDE), :, pl.ds(128 * j, 128)],
                        target.at[pl.ds(0, WIDE), j, pl.ds(0, NF), :],
                        sems.at[side, a, j],
                    )
                )
    for copy in copies:
        copy.start()

    fill_coarse(coarse, (y_up, y_dn), (e, cc, cs), [(x, x) for x in range(NC)])
    for t in range(TC):
        coarse.put_tile(coarse.u, NC, t, x_hi[coarse_place(0, t)])
        coarse.put_tile(coarse.c, NC, t, x_hi[coarse_place(1, t)])
    coarse.halo_end(0, lambda k, t: x_lo[coarse_place(k, t)], True)
    sweep([coarse], 3, 3 + NC, lambda slab, x: slab.first_plane(x))
    coarse.halo_end(5 + NC, lambda k, t: x_hi[coarse_place(k, t)], False)
    for level in range(1, STEPS):
        coarse.start_step(level)

        def act(slab, x, level=level):
            def emit(x, own):
                out_c[x - 3] = own

            slab.step_plane(level, x, emit if level == STEPS - 1 else None)

        sweep([coarse], level, 6 + NC - level, act)

    pieces = []
    for x in (0, 1, 2, 14, 15, 16):
        pieces.append(jnp.concatenate([coarse.u[x, j] for j in range(2)], axis=1))
    deep[...] = exact_dot(jnp.concatenate(pieces, 0), depth_table(0, (ZC, ZF)))
    for i in range(6):
        lift_plane(deep, 24 * i, lifted, i)

    for copy in copies:
        copy.wait()
    emits = []
    for side, message in ((0, x_lo), (1, x_hi)):
        fill_fine(slabs[side], (y_up, y_dn), None, (NF - WIDE) * side, WIDE)
        slabs[side].halo_end(0, lambda k, t, message=message: message[fine_place(k, t)], True)

        def emit(x, own, side=side):
            at = 6 - x if side else x - 3
            low, high = 3 * side + lax.div(at, 2), 3 * side + lax.div(at + 1, 2)
            edge[side, at] = own + lifted_plane(lifted, low, high)

        emits.append(emit)
    smooth(slabs, 3, 10, lambda k: k, lambda k: 10 - k, emits)

    restrict_plane(slabs[0], 0, WIDE, 1, grown, mixed, 0)
    restrict_plane(slabs[1], 6, 5, 7, grown, mixed, NC)
    result = exact_dot(mixed[...], 0.5 * depth_table(1, (ZF, ZC)))
    finish = []
    for side in range(2):
        edge_r[side, 0] = result[NC * side : NC * (side + 1)]
        pairs = ((edge, out, 4, NF), (edge_r, out_r, 1, NC))
        for a, (source, target, size, length) in enumerate(pairs):
            finish.append(
                pltpu.make_async_copy(
                    source.at[side],
                    target.at[pl.ds((length - size) * side, size)],
                    out_sems.at[2 * side + a],
                )
            )
    for copy in finish:
        copy.start()
    for copy in finish:
        copy.wait()


def outer(u, c, f, e, cc, cs, y_up, y_dn, x_lo, x_hi, mid, mid_r):
    anywhere = pl.BlockSpec(memory_space=pl.ANY)
    vmem = pl.BlockSpec(memory_space=pltpu.VMEM)
    return pl.pallas_call(
        outer_kernel,
        in_specs=[anywhere] * 3 + [vmem] * 7 + [anywhere] * 2,
        out_specs=[anywhere, anywhere, vmem],
        out_shape=[
            jax.ShapeDtypeStruct((NF, NF, ZF), F32),
            jax.ShapeDtypeStruct((NC, NC, ZC), F32),
            jax.ShapeDtypeStruct((NC, NC, ZC), F32),
        ],
        scratch_shapes=[
            pltpu.SemaphoreType.DMA((2, 3, 4)),
            pltpu.SemaphoreType.DMA((4,)),
            pltpu.VMEM((4, NF + 8, 128), F32),
            pltpu.VMEM((2 * NC, ZF), F32),
            pltpu.VMEM((24 * 6, ZF), F32),
            pltpu.VMEM((6, 4, NF, 128), F32),
            pltpu.VMEM((2, 4, NF, ZF), F32),
            pltpu.VMEM((2, 1, NC, ZC), F32),
        ]
        + (Slab.natural(WIDE + 1, TF, ZF) + Slab.work(WIDE + 3, TF, ZF)) * 2
        + Slab.natural(NC + 1, TC, ZC)
        + Slab.work(NC + 6, TC, ZC),
        compiler_params=pltpu.CompilerParams(vmem_limit_bytes=LIMIT),
        input_output_aliases={10: 0, 11: 1},
        name="outer_planes",
    )(u, c, f, e, cc, cs, y_up, y_dn, x_lo, x_hi, mid, mid_r)


def shift(block, axis, by):
    count = lax.axis_size(axis)
    return lax.ppermute(block, axis, [(i, (i + by) % count) for i in range(count)])


def local(u, f, c, e, cs, cc):
    y_up, y_dn = pack_y(u, c, f, e, cc, cs)
    y_up = shift(y_up, "gy", -1)
    y_dn = shift(y_dn, "gy", 1)
    x_lo, x_hi = pack_x(u, c, f, e, cc, cs, y_up, y_dn)
    from_hi = shift(x_lo, "gx", -1)
    from_lo = shift(x_hi, "gx", 1)
    mid, mid_r = inner(u, c, f, e, y_up, y_dn)
    return tuple(outer(u, c, f, e, cc, cs, y_up, y_dn, from_lo, from_hi, mid, mid_r))


def solution(mesh):
    placed = P("gx", "gy", None)
    return jax.shard_map(
        local,
        mesh=mesh,
        in_specs=(placed,) * 6,
        out_specs=(placed,) * 3,
        check_vma=False,
    )
```

time: 116 us -> 78.2 us (0.67)
  Pallas kernels: 58.8 us -> 41 us
  waiting for transfers between devices: 36.5 us -> 22 us
  starting transfers between devices: 18.7 us -> 11.3 us
  local copies, waits for them, and re-layouts: 1.34 us -> 3.06 us
    ppermute x6 -> x4, waiting for transfers between devices: 36.5 us -> 22 us  [shift(): lax.ppermute(block, axis, [(i, (i + by) % count) for i in range(count)])]
    pallas_call x2 -> x3, Pallas kernels: 32.3 us -> 22.4 us  [the longest x1 14.4 us: outer(): pl.pallas_call(outer_kernel, in_specs=[anywhere] * 3 + [vmem] * 7 + [anyw...]
    pallas_call x1, Pallas kernels: 26.5 us -> 18.5 us  [inner(): pl.pallas_call(inner_kernel, in_specs=[anywhere] * 3 + [vmem] * 3, out_sp...]
    ppermute x6 -> x4, starting transfers between devices: 18.7 us -> 11.3 us  [shift(): lax.ppermute(block, axis, [(i, (i + by) % count) for i in range(count)])]
    unnamed x19 -> x8, local copies, waits for them, and re-layouts: 1.34 us -> 3.06 us
  transfers between devices with their start and end apart: 6 -> 4, of which waited for: 1 -> 1; matrix products, arithmetic and copies ran while one was open for 0% -> 0% of each run, Pallas kernels for 23% -> 24%
where the time goes in v1:
time: 78.2 us; the launch traced here: 78 us
  Pallas kernels  41 us (52%)
  waiting for transfers between devices  22 us (28%)
  starting transfers between devices  11.3 us (14%)
  local copies, waits for them, and re-layouts  3.06 us (4%)
    ppermute x4, waiting for transfers between devices, shift(): lax.ppermute(block, axis, [(i, (i + by) % count) for i in range(count)])  22 us
    pallas_call x1, Pallas kernels, inner(): pl.pallas_call(inner_kernel, in_specs=[anywhere] * 3 + [vmem] * 3, out_sp...  18.5 us
    pallas_call x1, Pallas kernels, outer(): pl.pallas_call(outer_kernel, in_specs=[anywhere] * 3 + [vmem] * 7 + [anyw...  14.4 us
    ppermute x4, starting transfers between devices, shift(): lax.ppermute(block, axis, [(i, (i + by) % count) for i in range(count)])  11.3 us
    pallas_call x1, Pallas kernels, pack_x(): pl.pallas_call(pack_x_kernel, grid=(1,), in_specs=[face(0), face(1)] * 3...  4.44 us
    pallas_call x1, Pallas kernels, pack_y(): pl.pallas_call(pack_y_kernel, grid=(1,), in_specs=[strip(0), strip(3)] *...  3.6 us
    unnamed x8, local copies, waits for them, and re-layouts  3.06 us
  transfers between devices with their start and end apart: 4, of which 1 were waited for; matrix products, arithmetic and copies ran while one was open for 0% of the time, Pallas kernels for 24%

profile of v1, /device:TPU:1, one launch (start us, length us, event | category | flops | bytes accessed | tf_op | source)
XLA Modules:
  0.0 78.0 jit_solution(11793496598443496775)
XLA Ops:
  0.6 3.6 %pack_gy_faces.1 = (f32[480,512]{1,0:T(8,128)}, f32[480,512]{1,0:T(8,128)}) custom-call(f32[32,32,512]{2,1,0:T(8,128)} %u.3, f32[32,32,512]{2,1,0:T(8,128)} %u.3, f32[32,32,512]{2,1,0:T(8,128)} %c.3, f32[32,32,512]{2,1,0:T(8,128)} %c.3, f32[32,32,512]{2,1,0:T(8,128)} %f.3, f32[32,32,512]{2,1,0:T(8,128)} %f.3, f32[16,16,256]{2,1,0:T(8,128)} %e.7, ...), custom_call_target="tpu_custom_call" | custom-call | tf_op jit(solution)/shard_map/pack_gy_faces/pallas_call | solution.py:83
  4.2 3.2 %collective-permute-start = (f32[480,512]{1,0:T(8,128)}, f32[480,512]{1,0:T(8,128)S(1)}, u32[]{:S(2)}, u32[]{:S(2)}) collective-permute-start(f32[480,512]{1,0:T(8,128)} %get-tuple-element.9), channel_id=1, source_target_pairs={{0,15},{1,0},{2,1},{3,2},{4,3},{5,4},{6,5},{7,6},{8,7},{9,8},{10,9... | collective-permute-start | bytes 2949128 | tf_op jit(solution)/shard_map/ppermute | solution.py:669
  7.5 0.0 collective-permute-start.1
  7.5 22.0 %collective-permute-done.y_up = f32[480,512]{1,0:T(8,128)S(1)} collective-permute-done((f32[480,512]{1,0:T(8,128)}, f32[480,512]{1,0:T(8,128)S(1)}, u32[]{:S(2)}, u32[]{:S(2)}) %collective-permute-start) | collective-permute-done | bytes 983072 | tf_op jit(solution)/shard_map/ppermute | solution.py:669
  29.4 0.0 copy-start
  29.4 0.0 collective-permute-done.1.y_dn
  29.4 0.9 %copy-done = f32[480,512]{1,0:T(8,128)} copy-done((f32[480,512]{1,0:T(8,128)}, f32[480,512]{1,0:T(8,128)S(1)}, u32[]{:S(2)}) %copy-start) | copy-done | bytes 983064
  30.4 0.0 copy-start.1
  30.4 1.0 %copy-done.1 = f32[480,512]{1,0:T(8,128)} copy-done((f32[480,512]{1,0:T(8,128)}, f32[480,512]{1,0:T(8,128)S(1)}, u32[]{:S(2)}) %copy-start.1) | copy-done | bytes 983064
  31.4 4.4 %pack_gx_faces.1 = (f32[376,512]{1,0:T(8,128)}, f32[376,512]{1,0:T(8,128)}) custom-call(f32[32,32,512]{2,1,0:T(8,128)} %u.3, f32[32,32,512]{2,1,0:T(8,128)} %u.3, f32[32,32,512]{2,1,0:T(8,128)} %c.3, f32[32,32,512]{2,1,0:T(8,128)} %c.3, f32[32,32,512]{2,1,0:T(8,128)} %f.3, f32[32,32,512]{2,1,0:T(8,128)} %f.3, f32[16,16,256]{2,1,0:T(8,128)} %e.7, ...), custom_call_target="tpu_custom_call" | custom-call | tf_op jit(solution)/shard_map/pack_gx_faces/pallas_call | solution.py:536
  35.8 1.6 %collective-permute-start.2 = (f32[376,512]{1,0:T(8,128)}, f32[376,512]{1,0:T(8,128)S(1)}, u32[]{:S(2)}, u32[]{:S(2)}) collective-permute-start(f32[376,512]{1,0:T(8,128)} %get-tuple-element.11), channel_id=1, source_target_pairs={{0,16},{16,32},{32,48},{48,64},{64,80},{80,96},{96,112},{112,128},... | collective-permute-start | bytes 2310152 | tf_op jit(solution)/shard_map/ppermute | solution.py:669
  37.5 6.5 %collective-permute-start.3 = (f32[376,512]{1,0:T(8,128)}, f32[376,512]{1,0:T(8,128)S(1)}, u32[]{:S(2)}, u32[]{:S(2)}) collective-permute-start(f32[376,512]{1,0:T(8,128)} %get-tuple-element.12), channel_id=1, source_target_pairs={{0,240},{16,0},{32,16},{48,32},{64,48},{80,64},{96,80},{112,96},{1... | collective-permute-start | bytes 2310152 | tf_op jit(solution)/shard_map/ppermute | solution.py:669
  43.9 18.5 %inner_planes.1 = (f32[32,32,512]{2,1,0:T(8,128)}, f32[16,16,256]{2,1,0:T(8,128)}) custom-call(f32[32,32,512]{2,1,0:T(8,128)} %u.3, f32[32,32,512]{2,1,0:T(8,128)} %c.3, f32[32,32,512]{2,1,0:T(8,128)} %f.3, f32[16,16,256]{2,1,0:T(8,128)} %e.7, f32[480,512]{1,0:T(8,128)} %copy-done, f32[480,512]{1,0:T(8,128)} %copy-done.1), custom_call_target="tpu_custom_call" | custom-call | flops 30000001024 | bytes 12000000 | tf_op jit(solution)/shard_map/inner_planes/pallas_call | solution.py:423
  62.5 0.0 collective-permute-done.2.x_lo
  62.5 0.0 copy-start.2
  62.5 0.0 collective-permute-done.3.x_hi
  62.5 0.0 copy-start.3
  62.5 0.9 %copy-done.2 = f32[376,512]{1,0:T(8,128)} copy-done((f32[376,512]{1,0:T(8,128)}, f32[376,512]{1,0:T(8,128)S(1)}, u32[]{:S(2)}) %copy-start.2) | copy-done | bytes 770072
  63.4 0.2 copy-done.3
  63.6 14.4 %outer_planes.1 = (f32[32,32,512]{2,1,0:T(8,128)}, f32[16,16,256]{2,1,0:T(8,128)}, f32[16,16,256]{2,1,0:T(8,128)}) custom-call(f32[32,32,512]{2,1,0:T(8,128)} %u.3, f32[32,32,512]{2,1,0:T(8,128)} %c.3, f32[32,32,512]{2,1,0:T(8,128)} %f.3, f32[16,16,256]{2,1,0:T(8,128)} %e.7, f32[16,16,256]{2,1,0:T(8,128)} %cc.5, ...), custom_call_target="tpu_custom_call", output_to_operand_aliasing={{0}: (10, {}), {1}: (11, {})} | custom-call | tf_op jit(solution)/shard_map/outer_planes/pallas_call | solution.py:639
Async XLA Ops:
  4.2 25.2 %collective-permute-start = (f32[480,512]{1,0:T(8,128)}, f32[480,512]{1,0:T(8,128)S(1)}, u32[]{:S(2)}, u32[]{:S(2)}) collective-permute-start(f32[480,512]{1,0:T(8,128)} %get-tuple-element.9), channel_id=1, source_target_pairs={{0,15},{1,0},{2,1},{3,2},{4,3},{5,4},{6,5},{7,6},{8,7},{9,8},{10,9... | collective-permute-start | bytes 2949128 | tf_op jit(solution)/shard_map/ppermute | solution.py:669
  7.5 22.0 %collective-permute-start.1 = (f32[480,512]{1,0:T(8,128)}, f32[480,512]{1,0:T(8,128)S(1)}, u32[]{:S(2)}, u32[]{:S(2)}) collective-permute-start(f32[480,512]{1,0:T(8,128)} %get-tuple-element.10), channel_id=1, source_target_pairs={{0,1},{1,2},{2,3},{3,4},{4,5},{5,6},{6,7},{7,8},{8,9},{9,10},{10,1... | collective-permute-start | bytes 2949128 | tf_op jit(solution)/shard_map/ppermute | solution.py:669
  29.4 0.9 %copy-start = (f32[480,512]{1,0:T(8,128)}, f32[480,512]{1,0:T(8,128)S(1)}, u32[]{:S(2)}) copy-start(f32[480,512]{1,0:T(8,128)S(1)} %collective-permute-done.y_up) | copy-start | bytes 2949124
  30.4 1.0 %copy-start.1 = (f32[480,512]{1,0:T(8,128)}, f32[480,512]{1,0:T(8,128)S(1)}, u32[]{:S(2)}) copy-start(f32[480,512]{1,0:T(8,128)S(1)} %collective-permute-done.1.y_dn) | copy-start | bytes 2949124
  35.8 26.6 %collective-permute-start.2 = (f32[376,512]{1,0:T(8,128)}, f32[376,512]{1,0:T(8,128)S(1)}, u32[]{:S(2)}, u32[]{:S(2)}) collective-permute-start(f32[376,512]{1,0:T(8,128)} %get-tuple-element.11), channel_id=1, source_target_pairs={{0,16},{16,32},{32,48},{48,64},{64,80},{80,96},{96,112},{112,128},... | collective-permute-start | bytes 2310152 | tf_op jit(solution)/shard_map/ppermute | solution.py:669
  37.5 25.0 %collective-permute-start.3 = (f32[376,512]{1,0:T(8,128)}, f32[376,512]{1,0:T(8,128)S(1)}, u32[]{:S(2)}, u32[]{:S(2)}) collective-permute-start(f32[376,512]{1,0:T(8,128)} %get-tuple-element.12), channel_id=1, source_target_pairs={{0,240},{16,0},{32,16},{48,32},{64,48},{80,64},{96,80},{112,96},{1... | collective-permute-start | bytes 2310152 | tf_op jit(solution)/shard_map/ppermute | solution.py:669
  62.5 0.9 %copy-start.2 = (f32[376,512]{1,0:T(8,128)}, f32[376,512]{1,0:T(8,128)S(1)}, u32[]{:S(2)}) copy-start(f32[376,512]{1,0:T(8,128)S(1)} %collective-permute-done.2.x_lo) | copy-start | bytes 2310148
  62.5 1.1 %copy-start.3 = (f32[376,512]{1,0:T(8,128)}, f32[376,512]{1,0:T(8,128)S(1)}, u32[]{:S(2)}) copy-start(f32[376,512]{1,0:T(8,128)S(1)} %collective-permute-done.3.x_hi) | copy-start | bytes 2310148

commit v2 on v1

--- a/solution.py
+++ b/solution.py
@@ -16,7 +16,10 @@
 NC, ZC, TC = 16, 256, 3
 XROWS = 7 * 8 * TF + 4 * 8 * TC
 YROWS = 8 * (NF + NF // 2 + 12)
-LIMIT = 56 * 1024 * 1024
+LIMIT = 60 * 1024 * 1024
+PACK_LIMIT = 16 * 1024 * 1024
+INNER_LIMIT = 40 * 1024 * 1024
+OUTER_LIMIT = 32 * 1024 * 1024
 
 
 def step_factors():
@@ -223,27 +226,39 @@
                 self.flux[rows, :] = flux
                 self.put_tile(self.f, self.own, t, residual)
 
-    def first_plane(self, x):
+    def first_plane(self, x, known=None, more=False):
         half = 0.5 * self.scale
-        u, c = self.tiles(self.u, x), self.tiles(self.c, x)
+        every = range(self.t)
+        if known is None:
+            u, c = self.tiles(self.u, x), self.tiles(self.c, x)
+            fx_last = [self.flux[self.rows(t), :] for t in every]
+            wx_last = [self.wx[x - 1, self.rows(t), :] for t in every]
+        else:
+            u, c, fx_last, wx_last = known
+        u_next, c_next = self.tiles(self.u, x + 1), self.tiles(self.c, x + 1)
+        kept_fx, kept_wx = [], []
         wy, wy_last, wz, wz_last = self.cross_weights(c)
         cross = self.cross_flow(u, wy, wy_last, wz, wz_last)
         for t in range(self.t):
             rows = self.rows(t)
-            wx = half * (c[t] + self.tile(self.c, x + 1, t))
-            fx = wx * (self.tile(self.u, x + 1, t) - u[t])
-            faces = (wx + self.wx[x - 1, rows, :]) + (wy[t] + wy_last[t]) + (wz[t] + wz_last[t])
+            wx = half * (c[t] + c_next[t])
+            fx = wx * (u_next[t] - u[t])
+            faces = (wx + wx_last[t]) + (wy[t] + wy_last[t]) + (wz[t] + wz_last[t])
             inv = self.keep_weights(x, t, wy[t], wz[t], wz_last[t], faces)
-            flow = (fx - self.flux[rows, :]) + cross[t]
+            flow = (fx - fx_last[t]) + cross[t]
             residual = self.tile(self.f, x, t) - MASS * u[t] + flow
             q = residual * inv
             p = q * (1.0 / THETA)
-            self.flux[rows, :] = fx
+            kept_fx.append(fx)
+            kept_wx.append(wx)
+            if not more:
+                self.flux[rows, :] = fx
             self.wx[x, rows, :] = wx
             self.q[x, rows, :] = q
             self.p[x, rows, :] = p
             self.total[x, rows, :] = u[t] + p
             self.put_tile(self.f, self.at(x), t, residual)
+        return u_next, c_next, kept_fx, kept_wx
 
     def start_step(self, x):
         for t in range(self.t):
@@ -251,9 +266,16 @@
             change = self.p[x, rows, :] - self.p[x - 1, rows, :]
             self.flux[rows, :] = self.wx[x - 1, rows, :] * change
 
-    def step_plane(self, level, x, emit):
+    def step_plane(self, level, x, emit, known=None, more=False):
         keep, gain = step_factors()[level - 1]
-        p = [self.p[x, self.rows(t), :] for t in range(self.t)]
+        every = range(self.t)
+        if known is None:
+            p = [self.p[x, self.rows(t), :] for t in every]
+            fx_last = [self.flux[self.rows(t), :] for t in every]
+        else:
+            p, fx_last = known
+        p_next = [self.p[x + 1, self.rows(t), :] for t in every]
+        kept = []
         weights = [
             [ref[x, self.rows(t), :] for t in range(self.t)]
             for ref in (self.wy, self.wz, self.wz_last)
@@ -262,9 +284,11 @@
         cross = self.cross_flow(p, weights[0], wy_last, weights[1], weights[2])
         for t in range(self.t):
             rows = self.rows(t)
-            fx = self.wx[x, rows, :] * (self.p[x + 1, rows, :] - p[t])
-            flow = (fx - self.flux[rows, :]) + cross[t]
-            self.flux[rows, :] = fx
+            fx = self.wx[x, rows, :] * (p_next[t] - p[t])
+            flow = (fx - fx_last[t]) + cross[t]
+            kept.append(fx)
+            if not more:
+                self.flux[rows, :] = fx
             q = self.q[x, rows, :] + self.inv[x, rows, :] * (flow - MASS * p[t])
             new = keep * p[t] + gain * q
             total = self.total[x, rows, :] + new
@@ -280,28 +304,39 @@
             own = 8 * (self.t - 1)
             parts = [self.plane[j, 0:own, :] for j in range(self.lanes)]
             emit(x, jnp.concatenate(parts, axis=1))
-
-
-def sweep(slabs, low, high, act, unroll=2):
-    def body(x, carry):
+        return p_next, kept
+
+
+def sweep(slabs, low, high, act):
+    if (high - low) % 2:
         for slab in slabs:
-            act(slab, x)
+            act(slab, low, None, False)
+        low += 1
+
+    def body(i, carry):
+        x = low + 2 * i
+        known = [act(slab, x, None, True) for slab in slabs]
+        for slab, value in zip(slabs, known):
+            act(slab, x + 1, value, False)
         return carry
 
-    lax.fori_loop(low, high, body, 0, unroll=unroll)
-
-
-def smooth(slabs, first, last, low, high, emits, unroll=2):
-    sweep(slabs, first, last, lambda slab, x: slab.first_plane(x), unroll)
+    lax.fori_loop(0, (high - low) // 2, body, 0)
+
+
+def first_sweep(slabs, low, high):
+    sweep(slabs, low, high, lambda slab, x, known, more: slab.first_plane(x, known, more))
+
+
+def step_sweeps(slabs, low, high, emits):
     for level in range(1, STEPS):
         for slab in slabs:
             slab.start_step(low(level))
 
-        def act(slab, x, level=level):
+        def act(slab, x, known, more, level=level):
             emit = emits[slabs.index(slab)] if level == STEPS - 1 else None
-            slab.step_plane(level, x, emit)
-
-        sweep(slabs, low(level), high(level), act, unroll)
+            return slab.step_plane(level, x, emit, known, more)
+
+        sweep(slabs, low(level), high(level), act)
 
 
 def depth_table(coarse_axis, shape):
@@ -359,15 +394,16 @@
     sems, grown, mixed, deep, lifted = scratch[:5]
     slab = Slab(NF, TF, ZF, 1.0, scratch[5:8], scratch[8:])
     copies = []
-    for a, (source, target) in enumerate(((u, slab.u), (c, slab.c), (f, slab.f))):
-        for j in range(4):
-            copies.append(
-                pltpu.make_async_copy(
-                    source.at[:, :, pl.ds(128 * j, 128)],
-                    target.at[:, j, pl.ds(0, NF), :],
-                    sems.at[a, j],
+    for m in range(4):
+        for a, (source, target) in enumerate(((u, slab.u), (c, slab.c), (f, slab.f))):
+            for j in range(4):
+                copies.append(
+                    pltpu.make_async_copy(
+                        source.at[pl.ds(8 * m, 8), :, pl.ds(128 * j, 128)],
+                        target.at[pl.ds(8 * m, 8), j, pl.ds(0, NF), :],
+                        sems.at[m, a, j],
+                    )
                 )
-            )
     for copy in copies:
         copy.start()
 
@@ -382,9 +418,6 @@
         return carry
 
     lax.fori_loop(2, NC - 1, raise_one, 0)
-    for copy in copies:
-        copy.wait()
-
     def fill(m, carry):
         for half in range(2):
             x = 2 * m + half
@@ -403,8 +436,13 @@
     def emit(x, own):
         out[x] = own + lifted_plane(lifted, lax.div(x, 2), lax.div(x + 1, 2))
 
-    slab.open_end(0)
-    smooth([slab], 1, NF - 1, lambda k: 1 + k, lambda k: NF - 1 - k, [emit])
+    for m in range(4):
+        for copy in copies[12 * m : 12 * (m + 1)]:
+            copy.wait()
+        if m == 0:
+            slab.open_end(0)
+        first_sweep([slab], max(8 * m - 1, 1), 8 * m + 7)
+    step_sweeps([slab], lambda k: 1 + k, lambda k: NF - 1 - k, [emit])
 
     def lower(i, carry):
         row = pl.multiple_of(NC * (i - 1), 8)
@@ -429,7 +467,7 @@
             jax.ShapeDtypeStruct((NC, NC, ZC), F32),
         ],
         scratch_shapes=[
-            pltpu.SemaphoreType.DMA((3, 4)),
+            pltpu.SemaphoreType.DMA((4, 3, 4)),
             pltpu.VMEM((4, NF + 8, 128), F32),
             pltpu.VMEM((NC * (NC - 2), ZF), F32),
             pltpu.VMEM((24 * NC, ZF), F32),
@@ -437,7 +475,7 @@
         ]
         + Slab.natural(NF, TF, ZF)
         + Slab.work(NF, TF, ZF),
-        compiler_params=pltpu.CompilerParams(vmem_limit_bytes=LIMIT),
+        compiler_params=pltpu.CompilerParams(vmem_limit_bytes=INNER_LIMIT),
         cost_estimate=pl.CostEstimate(
             flops=30_000_000_000, bytes_accessed=12_000_000, transcendentals=0
         ),
@@ -477,46 +515,60 @@
     return slice(row, row + 8), slice(ZC * (k % 2), ZC * (k % 2 + 1))
 
 
-def fill_fine(slab, refs, blocks, first, planes):
-    y_up, y_dn = refs
+def fill_fine(slab, halo, blocks, first, planes):
+    up, down, up_f, down_f = halo
     for i in range(planes):
-        x = first + i
         if blocks is not None:
             for target, block in zip((slab.u, slab.c, slab.f), blocks):
                 slab.put_own(target, i, block[i])
-        pair = (y_up[8 * x : 8 * x + 8, :], y_dn[8 * x : 8 * x + 8, :])
+        pair = (up[8 * i : 8 * i + 8, :], down[8 * i : 8 * i + 8, :])
         slab.put_halo(slab.u, i, halo_first(*pair))
         slab.put_halo(slab.c, i, halo_second(*pair))
-        row = 8 * (NF + x // 2)
-        pair = (y_up[row : row + 8, :], y_dn[row : row + 8, :])
-        slab.put_halo(slab.f, i, (halo_second if x % 2 else halo_first)(*pair))
+        row = 8 * (i // 2)
+        pair = (up_f[row : row + 8, :], down_f[row : row + 8, :])
+        slab.put_halo(slab.f, i, (halo_second if i % 2 else halo_first)(*pair))
 
 
 def fill_coarse(slab, refs, fields, planes):
-    base = 8 * (NF + NF // 2)
     for x, place in planes:
         for target, source in zip((slab.u, slab.c, slab.f), fields):
             slab.put_own(target, place, source[x])
-        pair = coarse_halo(*refs, base, x)
+        pair = coarse_halo(*refs, 0, x)
         slab.put_halo(slab.u, place, halo_first(*pair))
         slab.put_halo(slab.c, place, halo_second(*pair))
-        pair = coarse_halo(*refs, base, NC + x // 2)
+        pair = coarse_halo(*refs, 0, NC + x // 2)
         slab.put_halo(slab.f, place, (halo_second if x % 2 else halo_first)(*pair))
 
 
-def pack_x_kernel(
-    u_lo, u_hi, c_lo, c_hi, f_lo, f_hi, e, cc, cs, y_up, y_dn, x_lo, x_hi, *scratch
-):
-    for side, blocks, out in ((0, (u_lo, c_lo, f_lo), x_lo), (1, (u_hi, c_hi, f_hi), x_hi)):
+def side_halos(planes):
+    specs = []
+    for side in range(2):
+        at = (NF // planes - 1) * side
+        for _ in range(2):
+            specs.append(pl.BlockSpec((8 * planes, ZF), lambda i, at=at: (at, 0)))
+        at += 2 * NF // planes
+        for _ in range(2):
+            specs.append(pl.BlockSpec((4 * planes, ZF), lambda i, at=at: (at, 0)))
+    return specs
+
+
+COARSE_HALO = pl.BlockSpec((8 * 12, ZF), lambda i: (4, 0))
+
+
+def pack_x_kernel(u_lo, u_hi, c_lo, c_hi, f_lo, f_hi, e, cc, cs, *refs):
+    halos, coarse_halos, outs = (refs[:4], refs[4:8]), refs[8:10], refs[10:12]
+    scratch = refs[12:]
+    for side, blocks in ((0, (u_lo, c_lo, f_lo)), (1, (u_hi, c_hi, f_hi))):
+        out = outs[side]
         slab = Slab(4, TF, ZF, 1.0, scratch[6 * side : 6 * side + 3], (), 0, side == 1)
-        fill_fine(slab, (y_up, y_dn), blocks, 28 * side, 4)
+        fill_fine(slab, halos[side], blocks, 28 * side, 4)
 
         def write_fine(k, t, value, out=out):
             out[fine_place(k, t)] = value
 
         first_planes(slab, write_fine)
         slab = Slab(4, TC, ZC, 0.25, scratch[6 * side + 3 : 6 * side + 6], (), 0, side == 1)
-        fill_coarse(slab, (y_up, y_dn), (e, cc, cs), [(12 * side + i, i) for i in range(4)])
+        fill_coarse(slab, coarse_halos, (e, cc, cs), [(12 * side + i, i) for i in range(4)])
 
         def write_coarse(k, t, value, out=out):
             out[coarse_place(k, t)] = value
@@ -531,26 +583,29 @@
         return pl.BlockSpec((4, NF, ZF), lambda i: (7 * side, 0, 0))
 
     whole = pl.BlockSpec((NC, NC, ZC), lambda i: (0, 0, 0))
-    y_spec = pl.BlockSpec((YROWS, ZF), lambda i: (0, 0))
     x_spec = pl.BlockSpec((XROWS, ZF), lambda i: (0, 0))
     return pl.pallas_call(
         pack_x_kernel,
         grid=(1,),
-        in_specs=[face(0), face(1)] * 3 + [whole] * 3 + [y_spec] * 2,
+        in_specs=[face(0), face(1)] * 3 + [whole] * 3 + side_halos(4) + [COARSE_HALO] * 2,
         out_specs=[x_spec, x_spec],
         out_shape=[jax.ShapeDtypeStruct((XROWS, ZF), F32)] * 2,
         scratch_shapes=(Slab.natural(4, TF, ZF) + Slab.natural(4, TC, ZC)) * 2,
-        compiler_params=pltpu.CompilerParams(vmem_limit_bytes=LIMIT),
+        compiler_params=pltpu.CompilerParams(vmem_limit_bytes=PACK_LIMIT),
         name="pack_gx_faces",
-    )(u, u, c, c, f, f, e, cc, cs, y_up, y_dn)
+    )(u, u, c, c, f, f, e, cc, cs, *[y_up, y_dn] * 5)
 
 
 WIDE = 8
 
 
 def outer_kernel(
-    u, c, f, e, cc, cs, y_up, y_dn, x_lo, x_hi, mid, mid_r, out, out_r, out_c, *scratch
+    u, c, f, e, cc, cs, *refs,
 ):
+    halos, coarse_halos, messages = (refs[:4], refs[4:8]), refs[8:10], refs[10:12]
+    x_lo, x_hi = messages
+    out, out_r, out_c = refs[14:17]
+    scratch = refs[17:]
     sems, out_sems, grown, mixed, deep, lifted, edge, edge_r = scratch[:8]
     slabs = []
     for side in range(2):
@@ -572,23 +627,18 @@
     for copy in copies:
         copy.start()
 
-    fill_coarse(coarse, (y_up, y_dn), (e, cc, cs), [(x, x) for x in range(NC)])
+    fill_coarse(coarse, coarse_halos, (e, cc, cs), [(x, x) for x in range(NC)])
     for t in range(TC):
         coarse.put_tile(coarse.u, NC, t, x_hi[coarse_place(0, t)])
         coarse.put_tile(coarse.c, NC, t, x_hi[coarse_place(1, t)])
     coarse.halo_end(0, lambda k, t: x_lo[coarse_place(k, t)], True)
-    sweep([coarse], 3, 3 + NC, lambda slab, x: slab.first_plane(x))
+    first_sweep([coarse], 3, 3 + NC)
     coarse.halo_end(5 + NC, lambda k, t: x_hi[coarse_place(k, t)], False)
-    for level in range(1, STEPS):
-        coarse.start_step(level)
-
-        def act(slab, x, level=level):
-            def emit(x, own):
-                out_c[x - 3] = own
-
-            slab.step_plane(level, x, emit if level == STEPS - 1 else None)
-
-        sweep([coarse], level, 6 + NC - level, act)
+
+    def emit_coarse(x, own):
+        out_c[x - 3] = own
+
+    step_sweeps([coarse], lambda k: k, lambda k: 6 + NC - k, [emit_coarse])
 
     pieces = []
     for x in (0, 1, 2, 14, 15, 16):
@@ -600,8 +650,8 @@
     for copy in copies:
         copy.wait()
     emits = []
-    for side, message in ((0, x_lo), (1, x_hi)):
-        fill_fine(slabs[side], (y_up, y_dn), None, (NF - WIDE) * side, WIDE)
+    for side, message in enumerate(messages):
+        fill_fine(slabs[side], halos[side], None, (NF - WIDE) * side, WIDE)
         slabs[side].halo_end(0, lambda k, t, message=message: message[fine_place(k, t)], True)
 
         def emit(x, own, side=side):
@@ -610,7 +660,8 @@
             edge[side, at] = own + lifted_plane(lifted, low, high)
 
         emits.append(emit)
-    smooth(slabs, 3, 10, lambda k: k, lambda k: 10 - k, emits)
+    first_sweep(slabs, 3, 10)
+    step_sweeps(slabs, lambda k: k, lambda k: 10 - k, emits)
 
     restrict_plane(slabs[0], 0, WIDE, 1, grown, mixed, 0)
     restrict_plane(slabs[1], 6, 5, 7, grown, mixed, NC)
@@ -635,11 +686,14 @@
 
 def outer(u, c, f, e, cc, cs, y_up, y_dn, x_lo, x_hi, mid, mid_r):
     anywhere = pl.BlockSpec(memory_space=pl.ANY)
-    vmem = pl.BlockSpec(memory_space=pltpu.VMEM)
+    whole = pl.BlockSpec((NC, NC, ZC), lambda i: (0, 0, 0))
+    x_spec = pl.BlockSpec((XROWS, ZF), lambda i: (0, 0))
+    halo_specs = side_halos(WIDE) + [COARSE_HALO] * 2
     return pl.pallas_call(
         outer_kernel,
-        in_specs=[anywhere] * 3 + [vmem] * 7 + [anywhere] * 2,
-        out_specs=[anywhere, anywhere, vmem],
+        grid=(1,),
+        in_specs=[anywhere] * 3 + [whole] * 3 + halo_specs + [x_spec] * 2 + [anywhere] * 2,
+        out_specs=[anywhere, anywhere, whole],
         out_shape=[
             jax.ShapeDtypeStruct((NF, NF, ZF), F32),
             jax.ShapeDtypeStruct((NC, NC, ZC), F32),
@@ -658,10 +712,10 @@
         + (Slab.natural(WIDE + 1, TF, ZF) + Slab.work(WIDE + 3, TF, ZF)) * 2
         + Slab.natural(NC + 1, TC, ZC)
         + Slab.work(NC + 6, TC, ZC),
-        compiler_params=pltpu.CompilerParams(vmem_limit_bytes=LIMIT),
-        input_output_aliases={10: 0, 11: 1},
+        compiler_params=pltpu.CompilerParams(vmem_limit_bytes=OUTER_LIMIT),
+        input_output_aliases={18: 0, 19: 1},
         name="outer_planes",
-    )(u, c, f, e, cc, cs, y_up, y_dn, x_lo, x_hi, mid, mid_r)
+    )(u, c, f, e, cc, cs, *[y_up, y_dn] * 5, x_lo, x_hi, mid, mid_r)
 
 
 def shift(block, axis, by):

time: 78.2 us -> 71.7 us (0.917)
  Pallas kernels: 41 us -> 33.8 us
    pallas_call x1, Pallas kernels: 4.44 us -> 1.09 us  [pack_x(): pl.pallas_call(pack_x_kernel, grid=(1,), in_specs=[face(0), face(1)] * 3...]
    pallas_call x1, Pallas kernels: 18.5 us -> 16.4 us  [inner(): pl.pallas_call(inner_kernel, in_specs=[anywhere] * 3 + [vmem] * 3, out_sp...]
    pallas_call x1, Pallas kernels: 14.4 us -> 12.6 us  [outer(): pl.pallas_call(outer_kernel, grid=(1,), in_specs=[anywhere] * 3 + [whole]...]
    unnamed x8 -> x16, local copies, waits for them, and re-layouts: 3.06 us -> 3.2 us
  transfers between devices with their start and end apart: 4 -> 4, of which waited for: 1 -> 1; matrix products, arithmetic and copies ran while one was open for 0% -> 0% of each run, Pallas kernels for 24% -> 23%
where the time goes in v2:
time: 71.7 us; the launch traced here: 71.5 us
  Pallas kernels  33.8 us (47%)
  waiting for transfers between devices  22 us (31%)
  starting transfers between devices  11.7 us (16%)
  local copies, waits for them, and re-layouts  3.2 us (4%)
  between operations  0.89 us (1%)
    ppermute x4, waiting for transfers between devices, shift(): lax.ppermute(block, axis, [(i, (i + by) % count) for i in range(count)])  22 us
    pallas_call x1, Pallas kernels, inner(): pl.pallas_call(inner_kernel, in_specs=[anywhere] * 3 + [vmem] * 3, out_sp...  16.4 us
    pallas_call x1, Pallas kernels, outer(): pl.pallas_call(outer_kernel, grid=(1,), in_specs=[anywhere] * 3 + [whole]...  12.6 us
    ppermute x4, starting transfers between devices, shift(): lax.ppermute(block, axis, [(i, (i + by) % count) for i in range(count)])  11.7 us
    pallas_call x1, Pallas kernels, pack_y(): pl.pallas_call(pack_y_kernel, grid=(1,), in_specs=[strip(0), strip(3)] *...  3.7 us
    unnamed x16, local copies, waits for them, and re-layouts  3.2 us
  transfers between devices with their start and end apart: 4, of which 1 were waited for; matrix products, arithmetic and copies ran while one was open for 0% of the time, Pallas kernels for 23%

profile of v2, /device:TPU:1, one launch (start us, length us, event | category | flops | bytes accessed | tf_op | source)
XLA Modules:
  0.0 71.5 jit_solution(2485254661113742959)
XLA Ops:
  0.6 0.0 copy-start.5
  0.6 0.0 copy-start
  0.7 0.0 copy-start.6
  0.7 0.0 copy-start.7
  0.7 3.7 %pack_gy_faces.1 = (f32[480,512]{1,0:T(8,128)}, f32[480,512]{1,0:T(8,128)}) custom-call(f32[32,32,512]{2,1,0:T(8,128)} %u.3, f32[32,32,512]{2,1,0:T(8,128)} %u.3, f32[32,32,512]{2,1,0:T(8,128)} %c.3, f32[32,32,512]{2,1,0:T(8,128)} %c.3, f32[32,32,512]{2,1,0:T(8,128)} %f.3, f32[32,32,512]{2,1,0:T(8,128)} %f.3, f32[16,16,256]{2,1,0:T(8,128)} %e.7, ...), custom_call_target="tpu_custom_call" | custom-call | tf_op jit(solution)/shard_map/pack_gy_faces/pallas_call | solution.py:86
  4.4 3.2 %collective-permute-start = (f32[480,512]{1,0:T(8,128)}, f32[480,512]{1,0:T(8,128)S(1)}, u32[]{:S(2)}, u32[]{:S(2)}) collective-permute-start(f32[480,512]{1,0:T(8,128)} %get-tuple-element.9), channel_id=1, source_target_pairs={{0,15},{1,0},{2,1},{3,2},{4,3},{5,4},{6,5},{7,6},{8,7},{9,8},{10,9... | collective-permute-start | bytes 2949128 | tf_op jit(solution)/shard_map/ppermute | solution.py:723
  7.6 0.0 collective-permute-start.1
  7.6 22.0 %collective-permute-done.refs_0_.refs_2_.refs_4_.refs_6_.refs_8_.y_up = f32[480,512]{1,0:T(8,128)S(1)} collective-permute-done((f32[480,512]{1,0:T(8,128)}, f32[480,512]{1,0:T(8,128)S(1)}, u32[]{:S(2)}, u32[]{:S(2)}) %collective-permute-start) | collective-permute-done | bytes 983072 | tf_op jit(solution)/shard_map/ppermute | solution.py:723
  29.6 0.0 collective-permute-done.1.refs_1_.refs_3_.refs_5_.refs_7_.refs_9_.y_dn
  29.6 0.0 copy-done.5
  29.6 0.0 copy-done
  29.6 0.0 copy-done.6
  29.6 0.0 copy-done.7
  29.6 0.0 copy-start.1
  29.6 1.6 %copy-done.1 = f32[32,32,512]{2,1,0:T(8,128)S(1)} copy-done((f32[32,32,512]{2,1,0:T(8,128)S(1)}, f32[32,32,512]{2,1,0:T(8,128)}, u32[]{:S(2)}) %copy-start.1) | copy-done | bytes 2097176
  31.2 0.0 copy-start.3
  31.2 1.6 %copy-done.3 = f32[32,32,512]{2,1,0:T(8,128)S(1)} copy-done((f32[32,32,512]{2,1,0:T(8,128)S(1)}, f32[32,32,512]{2,1,0:T(8,128)}, u32[]{:S(2)}) %copy-start.3) | copy-done | bytes 2097176
  32.8 0.0 copy-start.2
  32.8 0.0 copy-start.4
  32.8 1.1 %pack_gx_faces.1 = (f32[376,512]{1,0:T(8,128)S(1)}, f32[376,512]{1,0:T(8,128)S(1)}) custom-call(f32[32,32,512]{2,1,0:T(8,128)S(1)} %copy-done, f32[32,32,512]{2,1,0:T(8,128)S(1)} %copy-done, f32[32,32,512]{2,1,0:T(8,128)S(1)} %copy-done.1, f32[32,32,512]{2,1,0:T(8,128)S(1)} %copy-done.1, f32[32,32,512]{2,1,0:T(8,128)S(1)} %copy-done.3, ...), custom_call_target="tpu_custom_call" | custom-call | tf_op jit(solution)/shard_map/pack_gx_faces/pallas_call | solution.py:587
  33.9 1.7 %collective-permute-start.2 = (f32[376,512]{1,0:T(8,128)S(1)}, f32[376,512]{1,0:T(8,128)S(1)}, u32[]{:S(2)}, u32[]{:S(2)}) collective-permute-start(f32[376,512]{1,0:T(8,128)S(1)} %get-tuple-element.11), channel_id=1, source_target_pairs={{0,16},{16,32},{32,48},{48,64},{64,80},{80,96},{96,112},{112,128},... | collective-permute-start | bytes 2310152 | tf_op jit(solution)/shard_map/ppermute | solution.py:723
  35.6 6.7 %collective-permute-start.3 = (f32[376,512]{1,0:T(8,128)S(1)}, f32[376,512]{1,0:T(8,128)S(1)}, u32[]{:S(2)}, u32[]{:S(2)}) collective-permute-start(f32[376,512]{1,0:T(8,128)S(1)} %get-tuple-element.12), channel_id=1, source_target_pairs={{0,240},{16,0},{32,16},{48,32},{64,48},{80,64},{96,80},{112,96},{1... | collective-permute-start | bytes 2310152 | tf_op jit(solution)/shard_map/ppermute | solution.py:723
  42.3 0.0 copy-done.2
  42.3 0.0 copy-done.4
  42.3 16.4 %inner_planes.1 = (f32[32,32,512]{2,1,0:T(8,128)}, f32[16,16,256]{2,1,0:T(8,128)}) custom-call(f32[32,32,512]{2,1,0:T(8,128)S(1)} %copy-done, f32[32,32,512]{2,1,0:T(8,128)S(1)} %copy-done.2, f32[32,32,512]{2,1,0:T(8,128)S(1)} %copy-done.4, f32[16,16,256]{2,1,0:T(8,128)S(1)} %copy-done.5, ...), custom_call_target="tpu_custom_call" | custom-call | flops 30000001024 | bytes 12000000 | tf_op jit(solution)/shard_map/inner_planes/pallas_call | solution.py:461
  58.7 0.0 collective-permute-done.2.refs_10_
  58.7 0.0 collective-permute-done.3.refs_11_
  58.8 12.6 %outer_planes.1 = (f32[32,32,512]{2,1,0:T(8,128)}, f32[16,16,256]{2,1,0:T(8,128)}, f32[16,16,256]{2,1,0:T(8,128)}) custom-call(f32[32,32,512]{2,1,0:T(8,128)S(1)} %copy-done, f32[32,32,512]{2,1,0:T(8,128)S(1)} %copy-done.2, f32[32,32,512]{2,1,0:T(8,128)S(1)} %copy-done.4, ...), custom_call_target="tpu_custom_call", output_to_operand_aliasing={{0}: (18, {}), {1}: (19, {})} | custom-call | tf_op jit(solution)/shard_map/outer_planes/pallas_call | solution.py:692
Async XLA Ops:
  0.6 29.0 %copy-start.5 = (f32[16,16,256]{2,1,0:T(8,128)S(1)}, f32[16,16,256]{2,1,0:T(8,128)}, u32[]{:S(2)}) copy-start(f32[16,16,256]{2,1,0:T(8,128)} %e.7) | copy-start | bytes 786436
  0.6 28.9 %copy-start = (f32[32,32,512]{2,1,0:T(8,128)S(1)}, f32[32,32,512]{2,1,0:T(8,128)}, u32[]{:S(2)}) copy-start(f32[32,32,512]{2,1,0:T(8,128)} %u.3) | copy-start | bytes 6291460
  0.7 28.9 %copy-start.6 = (f32[16,16,256]{2,1,0:T(8,128)S(1)}, f32[16,16,256]{2,1,0:T(8,128)}, u32[]{:S(2)}) copy-start(f32[16,16,256]{2,1,0:T(8,128)} %cc.5) | copy-start | bytes 786436
  0.7 28.9 %copy-start.7 = (f32[16,16,256]{2,1,0:T(8,128)S(1)}, f32[16,16,256]{2,1,0:T(8,128)}, u32[]{:S(2)}) copy-start(f32[16,16,256]{2,1,0:T(8,128)} %cs.5) | copy-start | bytes 786436
  4.4 25.2 %collective-permute-start = (f32[480,512]{1,0:T(8,128)}, f32[480,512]{1,0:T(8,128)S(1)}, u32[]{:S(2)}, u32[]{:S(2)}) collective-permute-start(f32[480,512]{1,0:T(8,128)} %get-tuple-element.9), channel_id=1, source_target_pairs={{0,15},{1,0},{2,1},{3,2},{4,3},{5,4},{6,5},{7,6},{8,7},{9,8},{10,9... | collective-permute-start | bytes 2949128 | tf_op jit(solution)/shard_map/ppermute | solution.py:723
  7.6 22.0 %collective-permute-start.1 = (f32[480,512]{1,0:T(8,128)}, f32[480,512]{1,0:T(8,128)S(1)}, u32[]{:S(2)}, u32[]{:S(2)}) collective-permute-start(f32[480,512]{1,0:T(8,128)} %get-tuple-element.10), channel_id=1, source_target_pairs={{0,1},{1,2},{2,3},{3,4},{4,5},{5,6},{6,7},{7,8},{8,9},{9,10},{10,1... | collective-permute-start | bytes 2949128 | tf_op jit(solution)/shard_map/ppermute | solution.py:723
  29.6 1.6 %copy-start.1 = (f32[32,32,512]{2,1,0:T(8,128)S(1)}, f32[32,32,512]{2,1,0:T(8,128)}, u32[]{:S(2)}) copy-start(f32[32,32,512]{2,1,0:T(8,128)} %c.3) | copy-start | bytes 6291460
  31.2 1.6 %copy-start.3 = (f32[32,32,512]{2,1,0:T(8,128)S(1)}, f32[32,32,512]{2,1,0:T(8,128)}, u32[]{:S(2)}) copy-start(f32[32,32,512]{2,1,0:T(8,128)} %f.3) | copy-start | bytes 6291460
  32.8 9.5 %copy-start.2 = (f32[32,32,512]{2,1,0:T(8,128)S(1)}, f32[32,32,512]{2,1,0:T(8,128)}, u32[]{:S(2)}) copy-start(f32[32,32,512]{2,1,0:T(8,128)} %c.3) | copy-start | bytes 6291460
  32.8 9.5 %copy-start.4 = (f32[32,32,512]{2,1,0:T(8,128)S(1)}, f32[32,32,512]{2,1,0:T(8,128)}, u32[]{:S(2)}) copy-start(f32[32,32,512]{2,1,0:T(8,128)} %f.3) | copy-start | bytes 6291460
  33.9 24.8 %collective-permute-start.2 = (f32[376,512]{1,0:T(8,128)S(1)}, f32[376,512]{1,0:T(8,128)S(1)}, u32[]{:S(2)}, u32[]{:S(2)}) collective-permute-start(f32[376,512]{1,0:T(8,128)S(1)} %get-tuple-element.11), channel_id=1, source_target_pairs={{0,16},{16,32},{32,48},{48,64},{64,80},{80,96},{96,112},{112,128},... | collective-permute-start | bytes 2310152 | tf_op jit(solution)/shard_map/ppermute | solution.py:723
  35.6 23.1 %collective-permute-start.3 = (f32[376,512]{1,0:T(8,128)S(1)}, f32[376,512]{1,0:T(8,128)S(1)}, u32[]{:S(2)}, u32[]{:S(2)}) collective-permute-start(f32[376,512]{1,0:T(8,128)S(1)} %get-tuple-element.12), channel_id=1, source_target_pairs={{0,240},{16,0},{32,16},{48,32},{64,48},{80,64},{96,80},{112,96},{1... | collective-permute-start | bytes 2310152 | tf_op jit(solution)/shard_map/ppermute | solution.py:723

commit v3 on v2

--- a/solution.py
+++ b/solution.py
@@ -320,7 +320,7 @@
             act(slab, x + 1, value, False)
         return carry
 
-    lax.fori_loop(0, (high - low) // 2, body, 0)
+    lax.fori_loop(0, (high - low) // 2, body, 0, unroll=2)
 
 
 def first_sweep(slabs, low, high):

time: 71.7 us -> 68.7 us (0.958)
  Pallas kernels: 33.8 us -> 30.9 us
    pallas_call x1, Pallas kernels: 12.6 us -> 11.1 us  [outer(): pl.pallas_call(outer_kernel, grid=(1,), in_specs=[anywhere] * 3 + [whole]...]
    pallas_call x1, Pallas kernels: 16.4 us -> 14.9 us  [inner(): pl.pallas_call(inner_kernel, in_specs=[anywhere] * 3 + [vmem] * 3, out_sp...]
  transfers between devices with their start and end apart: 4 -> 4, of which waited for: 1 -> 1; matrix products, arithmetic and copies ran while one was open for 0% -> 0% of each run, Pallas kernels for 23% -> 22%
where the time goes in v3:
time: 68.7 us; the launch traced here: 68.6 us
  Pallas kernels  30.9 us (45%)
  waiting for transfers between devices  22 us (32%)
  starting transfers between devices  11.7 us (17%)
  local copies, waits for them, and re-layouts  3.2 us (5%)
  between operations  0.89 us (1%)
    ppermute x4, waiting for transfers between devices, shift(): lax.ppermute(block, axis, [(i, (i + by) % count) for i in range(count)])  22 us
    pallas_call x1, Pallas kernels, inner(): pl.pallas_call(inner_kernel, in_specs=[anywhere] * 3 + [vmem] * 3, out_sp...  14.9 us
    ppermute x4, starting transfers between devices, shift(): lax.ppermute(block, axis, [(i, (i + by) % count) for i in range(count)])  11.7 us
    pallas_call x1, Pallas kernels, outer(): pl.pallas_call(outer_kernel, grid=(1,), in_specs=[anywhere] * 3 + [whole]...  11.1 us
    pallas_call x1, Pallas kernels, pack_y(): pl.pallas_call(pack_y_kernel, grid=(1,), in_specs=[strip(0), strip(3)] *...  3.7 us
    unnamed x16, local copies, waits for them, and re-layouts  3.2 us
  transfers between devices with their start and end apart: 4, of which 1 were waited for; matrix products, arithmetic and copies ran while one was open for 0% of the time, Pallas kernels for 22%

profile of v3, /device:TPU:1, one launch (start us, length us, event | category | flops | bytes accessed | tf_op | source)
XLA Modules:
  0.0 68.6 jit_solution(8219166061915250897)
XLA Ops:
  0.6 0.0 copy-start.5
  0.6 0.0 copy-start
  0.7 0.0 copy-start.6
  0.7 0.0 copy-start.7
  0.7 3.7 %pack_gy_faces.1 = (f32[480,512]{1,0:T(8,128)}, f32[480,512]{1,0:T(8,128)}) custom-call(f32[32,32,512]{2,1,0:T(8,128)} %u.3, f32[32,32,512]{2,1,0:T(8,128)} %u.3, f32[32,32,512]{2,1,0:T(8,128)} %c.3, f32[32,32,512]{2,1,0:T(8,128)} %c.3, f32[32,32,512]{2,1,0:T(8,128)} %f.3, f32[32,32,512]{2,1,0:T(8,128)} %f.3, f32[16,16,256]{2,1,0:T(8,128)} %e.7, ...), custom_call_target="tpu_custom_call" | custom-call | tf_op jit(solution)/shard_map/pack_gy_faces/pallas_call | solution.py:86
  4.4 3.2 %collective-permute-start = (f32[480,512]{1,0:T(8,128)}, f32[480,512]{1,0:T(8,128)S(1)}, u32[]{:S(2)}, u32[]{:S(2)}) collective-permute-start(f32[480,512]{1,0:T(8,128)} %get-tuple-element.9), channel_id=1, source_target_pairs={{0,15},{1,0},{2,1},{3,2},{4,3},{5,4},{6,5},{7,6},{8,7},{9,8},{10,9... | collective-permute-start | bytes 2949128 | tf_op jit(solution)/shard_map/ppermute | solution.py:723
  7.6 0.0 collective-permute-start.1
  7.6 22.0 %collective-permute-done.refs_0_.refs_2_.refs_4_.refs_6_.refs_8_.y_up = f32[480,512]{1,0:T(8,128)S(1)} collective-permute-done((f32[480,512]{1,0:T(8,128)}, f32[480,512]{1,0:T(8,128)S(1)}, u32[]{:S(2)}, u32[]{:S(2)}) %collective-permute-start) | collective-permute-done | bytes 983072 | tf_op jit(solution)/shard_map/ppermute | solution.py:723
  29.6 0.0 collective-permute-done.1.refs_1_.refs_3_.refs_5_.refs_7_.refs_9_.y_dn
  29.6 0.0 copy-done.5
  29.6 0.0 copy-done
  29.6 0.0 copy-done.6
  29.6 0.0 copy-done.7
  29.6 0.0 copy-start.1
  29.6 1.6 %copy-done.1 = f32[32,32,512]{2,1,0:T(8,128)S(1)} copy-done((f32[32,32,512]{2,1,0:T(8,128)S(1)}, f32[32,32,512]{2,1,0:T(8,128)}, u32[]{:S(2)}) %copy-start.1) | copy-done | bytes 2097176
  31.2 0.0 copy-start.3
  31.2 1.6 %copy-done.3 = f32[32,32,512]{2,1,0:T(8,128)S(1)} copy-done((f32[32,32,512]{2,1,0:T(8,128)S(1)}, f32[32,32,512]{2,1,0:T(8,128)}, u32[]{:S(2)}) %copy-start.3) | copy-done | bytes 2097176
  32.8 0.0 copy-start.2
  32.8 0.0 copy-start.4
  32.8 1.1 %pack_gx_faces.1 = (f32[376,512]{1,0:T(8,128)S(1)}, f32[376,512]{1,0:T(8,128)S(1)}) custom-call(f32[32,32,512]{2,1,0:T(8,128)S(1)} %copy-done, f32[32,32,512]{2,1,0:T(8,128)S(1)} %copy-done, f32[32,32,512]{2,1,0:T(8,128)S(1)} %copy-done.1, f32[32,32,512]{2,1,0:T(8,128)S(1)} %copy-done.1, f32[32,32,512]{2,1,0:T(8,128)S(1)} %copy-done.3, ...), custom_call_target="tpu_custom_call" | custom-call | tf_op jit(solution)/shard_map/pack_gx_faces/pallas_call | solution.py:587
  33.9 1.7 %collective-permute-start.2 = (f32[376,512]{1,0:T(8,128)S(1)}, f32[376,512]{1,0:T(8,128)S(1)}, u32[]{:S(2)}, u32[]{:S(2)}) collective-permute-start(f32[376,512]{1,0:T(8,128)S(1)} %get-tuple-element.11), channel_id=1, source_target_pairs={{0,16},{16,32},{32,48},{48,64},{64,80},{80,96},{96,112},{112,128},... | collective-permute-start | bytes 2310152 | tf_op jit(solution)/shard_map/ppermute | solution.py:723
  35.6 6.7 %collective-permute-start.3 = (f32[376,512]{1,0:T(8,128)S(1)}, f32[376,512]{1,0:T(8,128)S(1)}, u32[]{:S(2)}, u32[]{:S(2)}) collective-permute-start(f32[376,512]{1,0:T(8,128)S(1)} %get-tuple-element.12), channel_id=1, source_target_pairs={{0,240},{16,0},{32,16},{48,32},{64,48},{80,64},{96,80},{112,96},{1... | collective-permute-start | bytes 2310152 | tf_op jit(solution)/shard_map/ppermute | solution.py:723
  42.3 0.0 copy-done.2
  42.3 0.0 copy-done.4
  42.3 14.9 %inner_planes.1 = (f32[32,32,512]{2,1,0:T(8,128)}, f32[16,16,256]{2,1,0:T(8,128)}) custom-call(f32[32,32,512]{2,1,0:T(8,128)S(1)} %copy-done, f32[32,32,512]{2,1,0:T(8,128)S(1)} %copy-done.2, f32[32,32,512]{2,1,0:T(8,128)S(1)} %copy-done.4, f32[16,16,256]{2,1,0:T(8,128)S(1)} %copy-done.5, ...), custom_call_target="tpu_custom_call" | custom-call | flops 30000001024 | bytes 12000000 | tf_op jit(solution)/shard_map/inner_planes/pallas_call | solution.py:461
  57.3 0.0 collective-permute-done.2.refs_10_
  57.3 0.0 collective-permute-done.3.refs_11_
  57.3 11.1 %outer_planes.1 = (f32[32,32,512]{2,1,0:T(8,128)}, f32[16,16,256]{2,1,0:T(8,128)}, f32[16,16,256]{2,1,0:T(8,128)}) custom-call(f32[32,32,512]{2,1,0:T(8,128)S(1)} %copy-done, f32[32,32,512]{2,1,0:T(8,128)S(1)} %copy-done.2, f32[32,32,512]{2,1,0:T(8,128)S(1)} %copy-done.4, ...), custom_call_target="tpu_custom_call", output_to_operand_aliasing={{0}: (18, {}), {1}: (19, {})} | custom-call | tf_op jit(solution)/shard_map/outer_planes/pallas_call | solution.py:692
Async XLA Ops:
  0.6 29.0 %copy-start.5 = (f32[16,16,256]{2,1,0:T(8,128)S(1)}, f32[16,16,256]{2,1,0:T(8,128)}, u32[]{:S(2)}) copy-start(f32[16,16,256]{2,1,0:T(8,128)} %e.7) | copy-start | bytes 786436
  0.6 28.9 %copy-start = (f32[32,32,512]{2,1,0:T(8,128)S(1)}, f32[32,32,512]{2,1,0:T(8,128)}, u32[]{:S(2)}) copy-start(f32[32,32,512]{2,1,0:T(8,128)} %u.3) | copy-start | bytes 6291460
  0.7 28.9 %copy-start.6 = (f32[16,16,256]{2,1,0:T(8,128)S(1)}, f32[16,16,256]{2,1,0:T(8,128)}, u32[]{:S(2)}) copy-start(f32[16,16,256]{2,1,0:T(8,128)} %cc.5) | copy-start | bytes 786436
  0.7 28.9 %copy-start.7 = (f32[16,16,256]{2,1,0:T(8,128)S(1)}, f32[16,16,256]{2,1,0:T(8,128)}, u32[]{:S(2)}) copy-start(f32[16,16,256]{2,1,0:T(8,128)} %cs.5) | copy-start | bytes 786436
  4.4 25.2 %collective-permute-start = (f32[480,512]{1,0:T(8,128)}, f32[480,512]{1,0:T(8,128)S(1)}, u32[]{:S(2)}, u32[]{:S(2)}) collective-permute-start(f32[480,512]{1,0:T(8,128)} %get-tuple-element.9), channel_id=1, source_target_pairs={{0,15},{1,0},{2,1},{3,2},{4,3},{5,4},{6,5},{7,6},{8,7},{9,8},{10,9... | collective-permute-start | bytes 2949128 | tf_op jit(solution)/shard_map/ppermute | solution.py:723
  7.6 22.0 %collective-permute-start.1 = (f32[480,512]{1,0:T(8,128)}, f32[480,512]{1,0:T(8,128)S(1)}, u32[]{:S(2)}, u32[]{:S(2)}) collective-permute-start(f32[480,512]{1,0:T(8,128)} %get-tuple-element.10), channel_id=1, source_target_pairs={{0,1},{1,2},{2,3},{3,4},{4,5},{5,6},{6,7},{7,8},{8,9},{9,10},{10,1... | collective-permute-start | bytes 2949128 | tf_op jit(solution)/shard_map/ppermute | solution.py:723
  29.6 1.6 %copy-start.1 = (f32[32,32,512]{2,1,0:T(8,128)S(1)}, f32[32,32,512]{2,1,0:T(8,128)}, u32[]{:S(2)}) copy-start(f32[32,32,512]{2,1,0:T(8,128)} %c.3) | copy-start | bytes 6291460
  31.2 1.6 %copy-start.3 = (f32[32,32,512]{2,1,0:T(8,128)S(1)}, f32[32,32,512]{2,1,0:T(8,128)}, u32[]{:S(2)}) copy-start(f32[32,32,512]{2,1,0:T(8,128)} %f.3) | copy-start | bytes 6291460
  32.8 9.5 %copy-start.2 = (f32[32,32,512]{2,1,0:T(8,128)S(1)}, f32[32,32,512]{2,1,0:T(8,128)}, u32[]{:S(2)}) copy-start(f32[32,32,512]{2,1,0:T(8,128)} %c.3) | copy-start | bytes 6291460
  32.8 9.5 %copy-start.4 = (f32[32,32,512]{2,1,0:T(8,128)S(1)}, f32[32,32,512]{2,1,0:T(8,128)}, u32[]{:S(2)}) copy-start(f32[32,32,512]{2,1,0:T(8,128)} %f.3) | copy-start | bytes 6291460
  33.9 23.4 %collective-permute-start.2 = (f32[376,512]{1,0:T(8,128)S(1)}, f32[376,512]{1,0:T(8,128)S(1)}, u32[]{:S(2)}, u32[]{:S(2)}) collective-permute-start(f32[376,512]{1,0:T(8,128)S(1)} %get-tuple-element.11), channel_id=1, source_target_pairs={{0,16},{16,32},{32,48},{48,64},{64,80},{80,96},{96,112},{112,128},... | collective-permute-start | bytes 2310152 | tf_op jit(solution)/shard_map/ppermute | solution.py:723
  35.6 21.7 %collective-permute-start.3 = (f32[376,512]{1,0:T(8,128)S(1)}, f32[376,512]{1,0:T(8,128)S(1)}, u32[]{:S(2)}, u32[]{:S(2)}) collective-permute-start(f32[376,512]{1,0:T(8,128)S(1)} %get-tuple-element.12), channel_id=1, source_target_pairs={{0,240},{16,0},{32,16},{48,32},{64,48},{80,64},{96,80},{112,96},{1... | collective-permute-start | bytes 2310152 | tf_op jit(solution)/shard_map/ppermute | solution.py:723
